TPU v7x, 512 devices: a whole 4x8x8 slice. The times are simulated.
512 devices in a mesh: ctx: 64 (over y, z_lo, core), tp: 8 (over x, z_hi).
Axes of the slice: x: 4, y: 8, z: 8 (z_hi: 2, z_lo: 4; z = z_hi * 4 + z_lo), core: 2. Of those that a mesh axis runs over, the one named last changes fastest.
Arguments:
- queries: bfloat16 [2, 8192, 8192], P(None, 'ctx', 'tp'), may hold values from -8 to 8
- keys: bfloat16 [2, 8192, 512], P(None, 'ctx'), may hold values from -8 to 8
- values: bfloat16 [2, 8192, 512], P(None, 'ctx'), may hold values from -6 to 6
- doc_lengths: int32 [16], replicated, may hold values from 1 to 4096, as said below
Outputs:
- attended: bfloat16 [2, 8192, 8192], P(None, 'ctx', 'tp')
- lse_gap: float32 [8192], P('ctx')
Inputs may be any that keep to these rules, and one draw needn't show every extreme that they name: `doc_lengths`: the rollout lengths sum to 8192; the first rollout is the longest, exactly 4096 tokens.
All inputs are finite; a program needn't handle non-finite values.
Results may differ from a plain program's by a relative error of at most 0.0045.
Values may be sent and summed in bfloat16 or wider, within the bound.
A program may use at most 64 MiB of HBM per device.

v0:
```python
import jax
import jax.numpy as jnp
from jax import lax
from jax.sharding import PartitionSpec as P

QH = 64
KVH = 4
HD = 128


masked_value = -1e30


def from_behind(array, axis, by):
    size = lax.axis_size(axis)
    pairs = [(i, i + by) for i in range(size) if 0 <= i + by < size]
    return lax.ppermute(array, axis, pairs)


def segment_ids(positions, doc_ends):
    return jnp.sum((positions[:, None] >= doc_ends[None, :]).astype(jnp.int32), axis=1)


def attend_tile(
    query_grid, key_block, value_block, query_pos, query_seg, block_start, doc_ends, state
):
    models, tok_rows, kv_local, repeats, head_dim = query_grid.shape
    key_rows = key_block.shape[1]
    key_pos = block_start + jnp.arange(key_rows, dtype=jnp.int32)
    key_seg = segment_ids(key_pos, doc_ends)
    visible = (query_seg[:, None] == key_seg[None, :]) & (query_pos[:, None] >= key_pos[None, :])
    key_grid = key_block.reshape(models, key_rows, kv_local, head_dim)
    value_grid = value_block.reshape(models, key_rows, kv_local, head_dim)
    scores = jnp.einsum(
        "mtcrd,mscd->mcrts", query_grid, key_grid, preferred_element_type=jnp.float32
    ) * head_dim ** (-0.5)
    scores = jnp.where(visible, scores, masked_value)
    running, totals, accum = state
    new_max = jnp.maximum(running, jnp.max(scores, axis=-1))
    weights = jnp.where(visible, jnp.exp(scores - new_max[..., None]), 0.0)
    factor = jnp.exp(running - new_max)
    totals = totals * factor + jnp.sum(weights, axis=-1)
    accum = accum * factor[..., None] + jnp.einsum(
        "mcrts,mscd->mcrtd",
        weights.astype(jnp.bfloat16),
        value_grid,
        preferred_element_type=jnp.float32,
    )
    return (new_max, totals, accum)


def per_device(queries, keys, values, doc_lengths):
    ctx_rank = lax.axis_index("ctx")
    ctx_count = lax.axis_size("ctx")
    tp_rank = lax.axis_index("tp")
    tok_rows = queries.shape[1]
    heads_here = queries.shape[2] // HD
    group_size = QH // KVH
    kv_local = max(heads_here // group_size, 1)
    repeats = heads_here // kv_local
    kv_first = tp_rank * heads_here // group_size
    own_keys = lax.dynamic_slice_in_dim(keys, kv_first * HD, kv_local * HD, 2)
    own_values = lax.dynamic_slice_in_dim(values, kv_first * HD, kv_local * HD, 2)
    query_grid = queries.reshape(2, tok_rows, kv_local, repeats, HD)
    doc_ends = jnp.cumsum(doc_lengths)
    query_pos = ctx_rank * tok_rows + jnp.arange(tok_rows, dtype=jnp.int32)
    query_seg = segment_ids(query_pos, doc_ends)

    def live(block):
        last_key = jnp.reshape(block * tok_rows + tok_rows - 1, (1,))
        return (block < ctx_rank) & (segment_ids(last_key, doc_ends)[0] == query_seg[0])

    def visit(grid, moving, block, state):

        def compute(current):
            return attend_tile(
                grid,
                moving[0],
                moving[1],
                query_pos,
                query_seg,
                block * tok_rows,
                doc_ends,
                current,
            )

        def keep(current):
            return current

        return lax.cond(live(block), compute, keep, state)

    start = (
        jnp.full((2, kv_local, repeats, tok_rows), masked_value, jnp.float32),
        jnp.zeros((2, kv_local, repeats, tok_rows), jnp.float32),
        jnp.zeros((2, kv_local, repeats, tok_rows, HD), jnp.float32),
    )
    state = attend_tile(
        query_grid, own_keys, own_values, query_pos, query_seg, ctx_rank * tok_rows, doc_ends, start
    )
    blocks = jnp.stack([own_keys, own_values])
    steps = ctx_count - 1

    def turn(step, carry):
        moving, current = carry
        moving = from_behind(moving, "ctx", 1)
        block = (ctx_rank - step) % ctx_count
        return (moving, visit(query_grid, moving, block, current))

    state = lax.fori_loop(1, steps + 1, turn, (blocks, state))[1]
    running, totals, accum = state
    attended = (
        (accum / totals[..., None])
        .transpose(0, 3, 1, 2, 4)
        .reshape(2, tok_rows, heads_here * HD)
        .astype(jnp.bfloat16)
    )
    log_norm = running + jnp.log(totals)
    gap_part = jnp.sum(log_norm[0] - log_norm[1], axis=(0, 1))
    lse_gap = lax.psum(gap_part, "tp") / QH
    return (attended, lse_gap)


def solution(mesh):
    in_specs = (P(None, "ctx", "tp"), P(None, "ctx", None), P(None, "ctx", None), P())
    out_specs = (P(None, "ctx", "tp"), P("ctx"))
    return jax.shard_map(
        per_device, mesh=mesh, in_specs=in_specs, out_specs=out_specs, check_vma=False
    )
```

profile of v0, /device:TPU:32, one launch (start us, length us, event | category | flops | bytes accessed | tf_op | source)
XLA Modules:
  0.0 687.6 jit_solution(11620592244546093024)
XLA Ops:
  5.6 644.3 %while.24 = (s32[]{:T(128)}, bf16[2,2,128,128]{3,2,1,0:T(8,128)(2,1)S(1)}, f32[2,1,8,128]{3,2,0,1:T(8,128)S(1)}, f32[2,1,8,128]{3,2,0,1:T(8,128)S(1)}, f32[2,1,8...) while((s32[]{:T(128)}, ...), condition=%wide.region_11.12_spmd.clone, body=%wide.region_4.11_spmd.clone.sunk | while | flops 137162944 | bytes 6887052 | solution.py:109
  8.9 6.9 %collective-permute-done = bf16[2,2,128,128]{3,2,1,0:T(8,128)(2,1)S(1)} collective-permute-done((bf16[2,2,128,128]{3,2,1,0:T(8,128)(2,1)S(1)}, bf16[2,2,128,128]{3,2,1,0:T(8,128)(2,1)S(1)}, u32[]{:S(2)}, u32[]{:S(2)}) %collective-permute-start) | collective-permute-done | bytes 131104 | tf_op jit(solution)/shard_map/while/body/eval_jaxpr/ppermute | solution.py:17
  19.1 6.9 %collective-permute-done = bf16[2,2,128,128]{3,2,1,0:T(8,128)(2,1)S(1)} collective-permute-done((bf16[2,2,128,128]{3,2,1,0:T(8,128)(2,1)S(1)}, bf16[2,2,128,128]{3,2,1,0:T(8,128)(2,1)S(1)}, u32[]{:S(2)}, u32[]{:S(2)}) %collective-permute-start) | collective-permute-done | bytes 131104 | tf_op jit(solution)/shard_map/while/body/eval_jaxpr/ppermute | solution.py:17
  29.4 6.9 %collective-permute-done = bf16[2,2,128,128]{3,2,1,0:T(8,128)(2,1)S(1)} collective-permute-done((bf16[2,2,128,128]{3,2,1,0:T(8,128)(2,1)S(1)}, bf16[2,2,128,128]{3,2,1,0:T(8,128)(2,1)S(1)}, u32[]{:S(2)}, u32[]{:S(2)}) %collective-permute-start) | collective-permute-done | bytes 131104 | tf_op jit(solution)/shard_map/while/body/eval_jaxpr/ppermute | solution.py:17
  39.6 6.9 %collective-permute-done = bf16[2,2,128,128]{3,2,1,0:T(8,128)(2,1)S(1)} collective-permute-done((bf16[2,2,128,128]{3,2,1,0:T(8,128)(2,1)S(1)}, bf16[2,2,128,128]{3,2,1,0:T(8,128)(2,1)S(1)}, u32[]{:S(2)}, u32[]{:S(2)}) %collective-permute-start) | collective-permute-done | bytes 131104 | tf_op jit(solution)/shard_map/while/body/eval_jaxpr/ppermute | solution.py:17
  49.8 6.9 %collective-permute-done = bf16[2,2,128,128]{3,2,1,0:T(8,128)(2,1)S(1)} collective-permute-done((bf16[2,2,128,128]{3,2,1,0:T(8,128)(2,1)S(1)}, bf16[2,2,128,128]{3,2,1,0:T(8,128)(2,1)S(1)}, u32[]{:S(2)}, u32[]{:S(2)}) %collective-permute-start) | collective-permute-done | bytes 131104 | tf_op jit(solution)/shard_map/while/body/eval_jaxpr/ppermute | solution.py:17
  60.1 6.9 %collective-permute-done = bf16[2,2,128,128]{3,2,1,0:T(8,128)(2,1)S(1)} collective-permute-done((bf16[2,2,128,128]{3,2,1,0:T(8,128)(2,1)S(1)}, bf16[2,2,128,128]{3,2,1,0:T(8,128)(2,1)S(1)}, u32[]{:S(2)}, u32[]{:S(2)}) %collective-permute-start) | collective-permute-done | bytes 131104 | tf_op jit(solution)/shard_map/while/body/eval_jaxpr/ppermute | solution.py:17
  70.3 6.9 %collective-permute-done = bf16[2,2,128,128]{3,2,1,0:T(8,128)(2,1)S(1)} collective-permute-done((bf16[2,2,128,128]{3,2,1,0:T(8,128)(2,1)S(1)}, bf16[2,2,128,128]{3,2,1,0:T(8,128)(2,1)S(1)}, u32[]{:S(2)}, u32[]{:S(2)}) %collective-permute-start) | collective-permute-done | bytes 131104 | tf_op jit(solution)/shard_map/while/body/eval_jaxpr/ppermute | solution.py:17
  80.5 6.9 %collective-permute-done = bf16[2,2,128,128]{3,2,1,0:T(8,128)(2,1)S(1)} collective-permute-done((bf16[2,2,128,128]{3,2,1,0:T(8,128)(2,1)S(1)}, bf16[2,2,128,128]{3,2,1,0:T(8,128)(2,1)S(1)}, u32[]{:S(2)}, u32[]{:S(2)}) %collective-permute-start) | collective-permute-done | bytes 131104 | tf_op jit(solution)/shard_map/while/body/eval_jaxpr/ppermute | solution.py:17
  90.7 6.9 %collective-permute-done = bf16[2,2,128,128]{3,2,1,0:T(8,128)(2,1)S(1)} collective-permute-done((bf16[2,2,128,128]{3,2,1,0:T(8,128)(2,1)S(1)}, bf16[2,2,128,128]{3,2,1,0:T(8,128)(2,1)S(1)}, u32[]{:S(2)}, u32[]{:S(2)}) %collective-permute-start) | collective-permute-done | bytes 131104 | tf_op jit(solution)/shard_map/while/body/eval_jaxpr/ppermute | solution.py:17
  101.0 6.9 %collective-permute-done = bf16[2,2,128,128]{3,2,1,0:T(8,128)(2,1)S(1)} collective-permute-done((bf16[2,2,128,128]{3,2,1,0:T(8,128)(2,1)S(1)}, bf16[2,2,128,128]{3,2,1,0:T(8,128)(2,1)S(1)}, u32[]{:S(2)}, u32[]{:S(2)}) %collective-permute-start) | collective-permute-done | bytes 131104 | tf_op jit(solution)/shard_map/while/body/eval_jaxpr/ppermute | solution.py:17
  111.2 6.9 %collective-permute-done = bf16[2,2,128,128]{3,2,1,0:T(8,128)(2,1)S(1)} collective-permute-done((bf16[2,2,128,128]{3,2,1,0:T(8,128)(2,1)S(1)}, bf16[2,2,128,128]{3,2,1,0:T(8,128)(2,1)S(1)}, u32[]{:S(2)}, u32[]{:S(2)}) %collective-permute-start) | collective-permute-done | bytes 131104 | tf_op jit(solution)/shard_map/while/body/eval_jaxpr/ppermute | solution.py:17
  121.4 6.9 %collective-permute-done = bf16[2,2,128,128]{3,2,1,0:T(8,128)(2,1)S(1)} collective-permute-done((bf16[2,2,128,128]{3,2,1,0:T(8,128)(2,1)S(1)}, bf16[2,2,128,128]{3,2,1,0:T(8,128)(2,1)S(1)}, u32[]{:S(2)}, u32[]{:S(2)}) %collective-permute-start) | collective-permute-done | bytes 131104 | tf_op jit(solution)/shard_map/while/body/eval_jaxpr/ppermute | solution.py:17
  131.6 6.9 %collective-permute-done = bf16[2,2,128,128]{3,2,1,0:T(8,128)(2,1)S(1)} collective-permute-done((bf16[2,2,128,128]{3,2,1,0:T(8,128)(2,1)S(1)}, bf16[2,2,128,128]{3,2,1,0:T(8,128)(2,1)S(1)}, u32[]{:S(2)}, u32[]{:S(2)}) %collective-permute-start) | collective-permute-done | bytes 131104 | tf_op jit(solution)/shard_map/while/body/eval_jaxpr/ppermute | solution.py:17
  141.9 6.9 %collective-permute-done = bf16[2,2,128,128]{3,2,1,0:T(8,128)(2,1)S(1)} collective-permute-done((bf16[2,2,128,128]{3,2,1,0:T(8,128)(2,1)S(1)}, bf16[2,2,128,128]{3,2,1,0:T(8,128)(2,1)S(1)}, u32[]{:S(2)}, u32[]{:S(2)}) %collective-permute-start) | collective-permute-done | bytes 131104 | tf_op jit(solution)/shard_map/while/body/eval_jaxpr/ppermute | solution.py:17
  152.1 6.9 %collective-permute-done = bf16[2,2,128,128]{3,2,1,0:T(8,128)(2,1)S(1)} collective-permute-done((bf16[2,2,128,128]{3,2,1,0:T(8,128)(2,1)S(1)}, bf16[2,2,128,128]{3,2,1,0:T(8,128)(2,1)S(1)}, u32[]{:S(2)}, u32[]{:S(2)}) %collective-permute-start) | collective-permute-done | bytes 131104 | tf_op jit(solution)/shard_map/while/body/eval_jaxpr/ppermute | solution.py:17
  162.3 6.9 %collective-permute-done = bf16[2,2,128,128]{3,2,1,0:T(8,128)(2,1)S(1)} collective-permute-done((bf16[2,2,128,128]{3,2,1,0:T(8,128)(2,1)S(1)}, bf16[2,2,128,128]{3,2,1,0:T(8,128)(2,1)S(1)}, u32[]{:S(2)}, u32[]{:S(2)}) %collective-permute-start) | collective-permute-done | bytes 131104 | tf_op jit(solution)/shard_map/while/body/eval_jaxpr/ppermute | solution.py:17
  172.5 6.9 %collective-permute-done = bf16[2,2,128,128]{3,2,1,0:T(8,128)(2,1)S(1)} collective-permute-done((bf16[2,2,128,128]{3,2,1,0:T(8,128)(2,1)S(1)}, bf16[2,2,128,128]{3,2,1,0:T(8,128)(2,1)S(1)}, u32[]{:S(2)}, u32[]{:S(2)}) %collective-permute-start) | collective-permute-done | bytes 131104 | tf_op jit(solution)/shard_map/while/body/eval_jaxpr/ppermute | solution.py:17
  182.8 6.9 %collective-permute-done = bf16[2,2,128,128]{3,2,1,0:T(8,128)(2,1)S(1)} collective-permute-done((bf16[2,2,128,128]{3,2,1,0:T(8,128)(2,1)S(1)}, bf16[2,2,128,128]{3,2,1,0:T(8,128)(2,1)S(1)}, u32[]{:S(2)}, u32[]{:S(2)}) %collective-permute-start) | collective-permute-done | bytes 131104 | tf_op jit(solution)/shard_map/while/body/eval_jaxpr/ppermute | solution.py:17
  193.0 6.9 %collective-permute-done = bf16[2,2,128,128]{3,2,1,0:T(8,128)(2,1)S(1)} collective-permute-done((bf16[2,2,128,128]{3,2,1,0:T(8,128)(2,1)S(1)}, bf16[2,2,128,128]{3,2,1,0:T(8,128)(2,1)S(1)}, u32[]{:S(2)}, u32[]{:S(2)}) %collective-permute-start) | collective-permute-done | bytes 131104 | tf_op jit(solution)/shard_map/while/body/eval_jaxpr/ppermute | solution.py:17
  203.2 6.9 %collective-permute-done = bf16[2,2,128,128]{3,2,1,0:T(8,128)(2,1)S(1)} collective-permute-done((bf16[2,2,128,128]{3,2,1,0:T(8,128)(2,1)S(1)}, bf16[2,2,128,128]{3,2,1,0:T(8,128)(2,1)S(1)}, u32[]{:S(2)}, u32[]{:S(2)}) %collective-permute-start) | collective-permute-done | bytes 131104 | tf_op jit(solution)/shard_map/while/body/eval_jaxpr/ppermute | solution.py:17
  213.5 6.9 %collective-permute-done = bf16[2,2,128,128]{3,2,1,0:T(8,128)(2,1)S(1)} collective-permute-done((bf16[2,2,128,128]{3,2,1,0:T(8,128)(2,1)S(1)}, bf16[2,2,128,128]{3,2,1,0:T(8,128)(2,1)S(1)}, u32[]{:S(2)}, u32[]{:S(2)}) %collective-permute-start) | collective-permute-done | bytes 131104 | tf_op jit(solution)/shard_map/while/body/eval_jaxpr/ppermute | solution.py:17
  223.7 6.9 %collective-permute-done = bf16[2,2,128,128]{3,2,1,0:T(8,128)(2,1)S(1)} collective-permute-done((bf16[2,2,128,128]{3,2,1,0:T(8,128)(2,1)S(1)}, bf16[2,2,128,128]{3,2,1,0:T(8,128)(2,1)S(1)}, u32[]{:S(2)}, u32[]{:S(2)}) %collective-permute-start) | collective-permute-done | bytes 131104 | tf_op jit(solution)/shard_map/while/body/eval_jaxpr/ppermute | solution.py:17
  233.9 6.9 %collective-permute-done = bf16[2,2,128,128]{3,2,1,0:T(8,128)(2,1)S(1)} collective-permute-done((bf16[2,2,128,128]{3,2,1,0:T(8,128)(2,1)S(1)}, bf16[2,2,128,128]{3,2,1,0:T(8,128)(2,1)S(1)}, u32[]{:S(2)}, u32[]{:S(2)}) %collective-permute-start) | collective-permute-done | bytes 131104 | tf_op jit(solution)/shard_map/while/body/eval_jaxpr/ppermute | solution.py:17
  244.1 6.9 %collective-permute-done = bf16[2,2,128,128]{3,2,1,0:T(8,128)(2,1)S(1)} collective-permute-done((bf16[2,2,128,128]{3,2,1,0:T(8,128)(2,1)S(1)}, bf16[2,2,128,128]{3,2,1,0:T(8,128)(2,1)S(1)}, u32[]{:S(2)}, u32[]{:S(2)}) %collective-permute-start) | collective-permute-done | bytes 131104 | tf_op jit(solution)/shard_map/while/body/eval_jaxpr/ppermute | solution.py:17
  254.4 6.9 %collective-permute-done = bf16[2,2,128,128]{3,2,1,0:T(8,128)(2,1)S(1)} collective-permute-done((bf16[2,2,128,128]{3,2,1,0:T(8,128)(2,1)S(1)}, bf16[2,2,128,128]{3,2,1,0:T(8,128)(2,1)S(1)}, u32[]{:S(2)}, u32[]{:S(2)}) %collective-permute-start) | collective-permute-done | bytes 131104 | tf_op jit(solution)/shard_map/while/body/eval_jaxpr/ppermute | solution.py:17
  264.6 6.9 %collective-permute-done = bf16[2,2,128,128]{3,2,1,0:T(8,128)(2,1)S(1)} collective-permute-done((bf16[2,2,128,128]{3,2,1,0:T(8,128)(2,1)S(1)}, bf16[2,2,128,128]{3,2,1,0:T(8,128)(2,1)S(1)}, u32[]{:S(2)}, u32[]{:S(2)}) %collective-permute-start) | collective-permute-done | bytes 131104 | tf_op jit(solution)/shard_map/while/body/eval_jaxpr/ppermute | solution.py:17
  274.8 6.9 %collective-permute-done = bf16[2,2,128,128]{3,2,1,0:T(8,128)(2,1)S(1)} collective-permute-done((bf16[2,2,128,128]{3,2,1,0:T(8,128)(2,1)S(1)}, bf16[2,2,128,128]{3,2,1,0:T(8,128)(2,1)S(1)}, u32[]{:S(2)}, u32[]{:S(2)}) %collective-permute-start) | collective-permute-done | bytes 131104 | tf_op jit(solution)/shard_map/while/body/eval_jaxpr/ppermute | solution.py:17
  285.0 6.9 %collective-permute-done = bf16[2,2,128,128]{3,2,1,0:T(8,128)(2,1)S(1)} collective-permute-done((bf16[2,2,128,128]{3,2,1,0:T(8,128)(2,1)S(1)}, bf16[2,2,128,128]{3,2,1,0:T(8,128)(2,1)S(1)}, u32[]{:S(2)}, u32[]{:S(2)}) %collective-permute-start) | collective-permute-done | bytes 131104 | tf_op jit(solution)/shard_map/while/body/eval_jaxpr/ppermute | solution.py:17
  295.3 6.9 %collective-permute-done = bf16[2,2,128,128]{3,2,1,0:T(8,128)(2,1)S(1)} collective-permute-done((bf16[2,2,128,128]{3,2,1,0:T(8,128)(2,1)S(1)}, bf16[2,2,128,128]{3,2,1,0:T(8,128)(2,1)S(1)}, u32[]{:S(2)}, u32[]{:S(2)}) %collective-permute-start) | collective-permute-done | bytes 131104 | tf_op jit(solution)/shard_map/while/body/eval_jaxpr/ppermute | solution.py:17
  305.5 6.9 %collective-permute-done = bf16[2,2,128,128]{3,2,1,0:T(8,128)(2,1)S(1)} collective-permute-done((bf16[2,2,128,128]{3,2,1,0:T(8,128)(2,1)S(1)}, bf16[2,2,128,128]{3,2,1,0:T(8,128)(2,1)S(1)}, u32[]{:S(2)}, u32[]{:S(2)}) %collective-permute-start) | collective-permute-done | bytes 131104 | tf_op jit(solution)/shard_map/while/body/eval_jaxpr/ppermute | solution.py:17
  315.7 6.9 %collective-permute-done = bf16[2,2,128,128]{3,2,1,0:T(8,128)(2,1)S(1)} collective-permute-done((bf16[2,2,128,128]{3,2,1,0:T(8,128)(2,1)S(1)}, bf16[2,2,128,128]{3,2,1,0:T(8,128)(2,1)S(1)}, u32[]{:S(2)}, u32[]{:S(2)}) %collective-permute-start) | collective-permute-done | bytes 131104 | tf_op jit(solution)/shard_map/while/body/eval_jaxpr/ppermute | solution.py:17
  326.0 6.9 %collective-permute-done = bf16[2,2,128,128]{3,2,1,0:T(8,128)(2,1)S(1)} collective-permute-done((bf16[2,2,128,128]{3,2,1,0:T(8,128)(2,1)S(1)}, bf16[2,2,128,128]{3,2,1,0:T(8,128)(2,1)S(1)}, u32[]{:S(2)}, u32[]{:S(2)}) %collective-permute-start) | collective-permute-done | bytes 131104 | tf_op jit(solution)/shard_map/while/body/eval_jaxpr/ppermute | solution.py:17
  377.1 6.9 %collective-permute-done = bf16[2,2,128,128]{3,2,1,0:T(8,128)(2,1)S(1)} collective-permute-done((bf16[2,2,128,128]{3,2,1,0:T(8,128)(2,1)S(1)}, bf16[2,2,128,128]{3,2,1,0:T(8,128)(2,1)S(1)}, u32[]{:S(2)}, u32[]{:S(2)}) %collective-permute-start) | collective-permute-done | bytes 131104 | tf_op jit(solution)/shard_map/while/body/eval_jaxpr/ppermute | solution.py:17
  387.3 6.9 %collective-permute-done = bf16[2,2,128,128]{3,2,1,0:T(8,128)(2,1)S(1)} collective-permute-done((bf16[2,2,128,128]{3,2,1,0:T(8,128)(2,1)S(1)}, bf16[2,2,128,128]{3,2,1,0:T(8,128)(2,1)S(1)}, u32[]{:S(2)}, u32[]{:S(2)}) %collective-permute-start) | collective-permute-done | bytes 131104 | tf_op jit(solution)/shard_map/while/body/eval_jaxpr/ppermute | solution.py:17
  397.5 6.9 %collective-permute-done = bf16[2,2,128,128]{3,2,1,0:T(8,128)(2,1)S(1)} collective-permute-done((bf16[2,2,128,128]{3,2,1,0:T(8,128)(2,1)S(1)}, bf16[2,2,128,128]{3,2,1,0:T(8,128)(2,1)S(1)}, u32[]{:S(2)}, u32[]{:S(2)}) %collective-permute-start) | collective-permute-done | bytes 131104 | tf_op jit(solution)/shard_map/while/body/eval_jaxpr/ppermute | solution.py:17
  407.8 6.9 %collective-permute-done = bf16[2,2,128,128]{3,2,1,0:T(8,128)(2,1)S(1)} collective-permute-done((bf16[2,2,128,128]{3,2,1,0:T(8,128)(2,1)S(1)}, bf16[2,2,128,128]{3,2,1,0:T(8,128)(2,1)S(1)}, u32[]{:S(2)}, u32[]{:S(2)}) %collective-permute-start) | collective-permute-done | bytes 131104 | tf_op jit(solution)/shard_map/while/body/eval_jaxpr/ppermute | solution.py:17
  418.0 6.9 %collective-permute-done = bf16[2,2,128,128]{3,2,1,0:T(8,128)(2,1)S(1)} collective-permute-done((bf16[2,2,128,128]{3,2,1,0:T(8,128)(2,1)S(1)}, bf16[2,2,128,128]{3,2,1,0:T(8,128)(2,1)S(1)}, u32[]{:S(2)}, u32[]{:S(2)}) %collective-permute-start) | collective-permute-done | bytes 131104 | tf_op jit(solution)/shard_map/while/body/eval_jaxpr/ppermute | solution.py:17
  479.4 6.9 %collective-permute-done = bf16[2,2,128,128]{3,2,1,0:T(8,128)(2,1)S(1)} collective-permute-done((bf16[2,2,128,128]{3,2,1,0:T(8,128)(2,1)S(1)}, bf16[2,2,128,128]{3,2,1,0:T(8,128)(2,1)S(1)}, u32[]{:S(2)}, u32[]{:S(2)}) %collective-permute-start) | collective-permute-done | bytes 131104 | tf_op jit(solution)/shard_map/while/body/eval_jaxpr/ppermute | solution.py:17
  489.6 6.9 %collective-permute-done = bf16[2,2,128,128]{3,2,1,0:T(8,128)(2,1)S(1)} collective-permute-done((bf16[2,2,128,128]{3,2,1,0:T(8,128)(2,1)S(1)}, bf16[2,2,128,128]{3,2,1,0:T(8,128)(2,1)S(1)}, u32[]{:S(2)}, u32[]{:S(2)}) %collective-permute-start) | collective-permute-done | bytes 131104 | tf_op jit(solution)/shard_map/while/body/eval_jaxpr/ppermute | solution.py:17
  499.8 6.9 %collective-permute-done = bf16[2,2,128,128]{3,2,1,0:T(8,128)(2,1)S(1)} collective-permute-done((bf16[2,2,128,128]{3,2,1,0:T(8,128)(2,1)S(1)}, bf16[2,2,128,128]{3,2,1,0:T(8,128)(2,1)S(1)}, u32[]{:S(2)}, u32[]{:S(2)}) %collective-permute-start) | collective-permute-done | bytes 131104 | tf_op jit(solution)/shard_map/while/body/eval_jaxpr/ppermute | solution.py:17
  510.0 6.9 %collective-permute-done = bf16[2,2,128,128]{3,2,1,0:T(8,128)(2,1)S(1)} collective-permute-done((bf16[2,2,128,128]{3,2,1,0:T(8,128)(2,1)S(1)}, bf16[2,2,128,128]{3,2,1,0:T(8,128)(2,1)S(1)}, u32[]{:S(2)}, u32[]{:S(2)}) %collective-permute-start) | collective-permute-done | bytes 131104 | tf_op jit(solution)/shard_map/while/body/eval_jaxpr/ppermute | solution.py:17
  571.4 6.9 %collective-permute-done = bf16[2,2,128,128]{3,2,1,0:T(8,128)(2,1)S(1)} collective-permute-done((bf16[2,2,128,128]{3,2,1,0:T(8,128)(2,1)S(1)}, bf16[2,2,128,128]{3,2,1,0:T(8,128)(2,1)S(1)}, u32[]{:S(2)}, u32[]{:S(2)}) %collective-permute-start) | collective-permute-done | bytes 131104 | tf_op jit(solution)/shard_map/while/body/eval_jaxpr/ppermute | solution.py:17
  581.6 6.9 %collective-permute-done = bf16[2,2,128,128]{3,2,1,0:T(8,128)(2,1)S(1)} collective-permute-done((bf16[2,2,128,128]{3,2,1,0:T(8,128)(2,1)S(1)}, bf16[2,2,128,128]{3,2,1,0:T(8,128)(2,1)S(1)}, u32[]{:S(2)}, u32[]{:S(2)}) %collective-permute-start) | collective-permute-done | bytes 131104 | tf_op jit(solution)/shard_map/while/body/eval_jaxpr/ppermute | solution.py:17
  591.8 6.9 %collective-permute-done = bf16[2,2,128,128]{3,2,1,0:T(8,128)(2,1)S(1)} collective-permute-done((bf16[2,2,128,128]{3,2,1,0:T(8,128)(2,1)S(1)}, bf16[2,2,128,128]{3,2,1,0:T(8,128)(2,1)S(1)}, u32[]{:S(2)}, u32[]{:S(2)}) %collective-permute-start) | collective-permute-done | bytes 131104 | tf_op jit(solution)/shard_map/while/body/eval_jaxpr/ppermute | solution.py:17
  602.1 6.9 %collective-permute-done = bf16[2,2,128,128]{3,2,1,0:T(8,128)(2,1)S(1)} collective-permute-done((bf16[2,2,128,128]{3,2,1,0:T(8,128)(2,1)S(1)}, bf16[2,2,128,128]{3,2,1,0:T(8,128)(2,1)S(1)}, u32[]{:S(2)}, u32[]{:S(2)}) %collective-permute-start) | collective-permute-done | bytes 131104 | tf_op jit(solution)/shard_map/while/body/eval_jaxpr/ppermute | solution.py:17
  612.3 6.9 %collective-permute-done = bf16[2,2,128,128]{3,2,1,0:T(8,128)(2,1)S(1)} collective-permute-done((bf16[2,2,128,128]{3,2,1,0:T(8,128)(2,1)S(1)}, bf16[2,2,128,128]{3,2,1,0:T(8,128)(2,1)S(1)}, u32[]{:S(2)}, u32[]{:S(2)}) %collective-permute-start) | collective-permute-done | bytes 131104 | tf_op jit(solution)/shard_map/while/body/eval_jaxpr/ppermute | solution.py:17
  650.0 35.4 %psum.7 = f32[128]{0:T(128)S(1)} all-reduce(f32[128]{0:T(128)S(1)} %fusion.37), channel_id=1, replica_groups=mesh['ctx'=64,'tp'=8] {'tp'}, use_global_device_ids=true, to_apply=%region_13.14 | all-reduce | flops 128 | bytes 1024 | tf_op jit(solution)/shard_map/psum | solution.py:119
  (359 shorter events, 288.3 us)
Async XLA Ops:
  5.7 10.2 %collective-permute-start = (bf16[2,2,128,128]{3,2,1,0:T(8,128)(2,1)S(1)}, bf16[2,2,128,128]{3,2,1,0:T(8,128)(2,1)S(1)}, u32[]{:S(2)}, u32[]{:S(2)}) collective-permute-start(bf16[2,2,128,128]{3,2,1,0:T(8,128)(2,1)S(1)} %get-tuple-element.556), channel_id=1, source_target_pairs={{0,8},{8,16},{16,24},{24,32},{32,40},{40,48},{48,56},{56,64},{64,7... | collective-permute-start | bytes 393224 | tf_op jit(solution)/shard_map/while/body/eval_jaxpr/ppermute | solution.py:17
  15.9 10.2 %collective-permute-start = (bf16[2,2,128,128]{3,2,1,0:T(8,128)(2,1)S(1)}, bf16[2,2,128,128]{3,2,1,0:T(8,128)(2,1)S(1)}, u32[]{:S(2)}, u32[]{:S(2)}) collective-permute-start(bf16[2,2,128,128]{3,2,1,0:T(8,128)(2,1)S(1)} %get-tuple-element.556), channel_id=1, source_target_pairs={{0,8},{8,16},{16,24},{24,32},{32,40},{40,48},{48,56},{56,64},{64,7... | collective-permute-start | bytes 393224 | tf_op jit(solution)/shard_map/while/body/eval_jaxpr/ppermute | solution.py:17
  26.1 10.2 %collective-permute-start = (bf16[2,2,128,128]{3,2,1,0:T(8,128)(2,1)S(1)}, bf16[2,2,128,128]{3,2,1,0:T(8,128)(2,1)S(1)}, u32[]{:S(2)}, u32[]{:S(2)}) collective-permute-start(bf16[2,2,128,128]{3,2,1,0:T(8,128)(2,1)S(1)} %get-tuple-element.556), channel_id=1, source_target_pairs={{0,8},{8,16},{16,24},{24,32},{32,40},{40,48},{48,56},{56,64},{64,7... | collective-permute-start | bytes 393224 | tf_op jit(solution)/shard_map/while/body/eval_jaxpr/ppermute | solution.py:17
  36.3 10.2 %collective-permute-start = (bf16[2,2,128,128]{3,2,1,0:T(8,128)(2,1)S(1)}, bf16[2,2,128,128]{3,2,1,0:T(8,128)(2,1)S(1)}, u32[]{:S(2)}, u32[]{:S(2)}) collective-permute-start(bf16[2,2,128,128]{3,2,1,0:T(8,128)(2,1)S(1)} %get-tuple-element.556), channel_id=1, source_target_pairs={{0,8},{8,16},{16,24},{24,32},{32,40},{40,48},{48,56},{56,64},{64,7... | collective-permute-start | bytes 393224 | tf_op jit(solution)/shard_map/while/body/eval_jaxpr/ppermute | solution.py:17
  46.6 10.2 %collective-permute-start = (bf16[2,2,128,128]{3,2,1,0:T(8,128)(2,1)S(1)}, bf16[2,2,128,128]{3,2,1,0:T(8,128)(2,1)S(1)}, u32[]{:S(2)}, u32[]{:S(2)}) collective-permute-start(bf16[2,2,128,128]{3,2,1,0:T(8,128)(2,1)S(1)} %get-tuple-element.556), channel_id=1, source_target_pairs={{0,8},{8,16},{16,24},{24,32},{32,40},{40,48},{48,56},{56,64},{64,7... | collective-permute-start | bytes 393224 | tf_op jit(solution)/shard_map/while/body/eval_jaxpr/ppermute | solution.py:17
  56.8 10.2 %collective-permute-start = (bf16[2,2,128,128]{3,2,1,0:T(8,128)(2,1)S(1)}, bf16[2,2,128,128]{3,2,1,0:T(8,128)(2,1)S(1)}, u32[]{:S(2)}, u32[]{:S(2)}) collective-permute-start(bf16[2,2,128,128]{3,2,1,0:T(8,128)(2,1)S(1)} %get-tuple-element.556), channel_id=1, source_target_pairs={{0,8},{8,16},{16,24},{24,32},{32,40},{40,48},{48,56},{56,64},{64,7... | collective-permute-start | bytes 393224 | tf_op jit(solution)/shard_map/while/body/eval_jaxpr/ppermute | solution.py:17
  67.0 10.2 %collective-permute-start = (bf16[2,2,128,128]{3,2,1,0:T(8,128)(2,1)S(1)}, bf16[2,2,128,128]{3,2,1,0:T(8,128)(2,1)S(1)}, u32[]{:S(2)}, u32[]{:S(2)}) collective-permute-start(bf16[2,2,128,128]{3,2,1,0:T(8,128)(2,1)S(1)} %get-tuple-element.556), channel_id=1, source_target_pairs={{0,8},{8,16},{16,24},{24,32},{32,40},{40,48},{48,56},{56,64},{64,7... | collective-permute-start | bytes 393224 | tf_op jit(solution)/shard_map/while/body/eval_jaxpr/ppermute | solution.py:17
  77.2 10.2 %collective-permute-start = (bf16[2,2,128,128]{3,2,1,0:T(8,128)(2,1)S(1)}, bf16[2,2,128,128]{3,2,1,0:T(8,128)(2,1)S(1)}, u32[]{:S(2)}, u32[]{:S(2)}) collective-permute-start(bf16[2,2,128,128]{3,2,1,0:T(8,128)(2,1)S(1)} %get-tuple-element.556), channel_id=1, source_target_pairs={{0,8},{8,16},{16,24},{24,32},{32,40},{40,48},{48,56},{56,64},{64,7... | collective-permute-start | bytes 393224 | tf_op jit(solution)/shard_map/while/body/eval_jaxpr/ppermute | solution.py:17
  87.5 10.2 %collective-permute-start = (bf16[2,2,128,128]{3,2,1,0:T(8,128)(2,1)S(1)}, bf16[2,2,128,128]{3,2,1,0:T(8,128)(2,1)S(1)}, u32[]{:S(2)}, u32[]{:S(2)}) collective-permute-start(bf16[2,2,128,128]{3,2,1,0:T(8,128)(2,1)S(1)} %get-tuple-element.556), channel_id=1, source_target_pairs={{0,8},{8,16},{16,24},{24,32},{32,40},{40,48},{48,56},{56,64},{64,7... | collective-permute-start | bytes 393224 | tf_op jit(solution)/shard_map/while/body/eval_jaxpr/ppermute | solution.py:17
  97.7 10.2 %collective-permute-start = (bf16[2,2,128,128]{3,2,1,0:T(8,128)(2,1)S(1)}, bf16[2,2,128,128]{3,2,1,0:T(8,128)(2,1)S(1)}, u32[]{:S(2)}, u32[]{:S(2)}) collective-permute-start(bf16[2,2,128,128]{3,2,1,0:T(8,128)(2,1)S(1)} %get-tuple-element.556), channel_id=1, source_target_pairs={{0,8},{8,16},{16,24},{24,32},{32,40},{40,48},{48,56},{56,64},{64,7... | collective-permute-start | bytes 393224 | tf_op jit(solution)/shard_map/while/body/eval_jaxpr/ppermute | solution.py:17
  107.9 10.2 %collective-permute-start = (bf16[2,2,128,128]{3,2,1,0:T(8,128)(2,1)S(1)}, bf16[2,2,128,128]{3,2,1,0:T(8,128)(2,1)S(1)}, u32[]{:S(2)}, u32[]{:S(2)}) collective-permute-start(bf16[2,2,128,128]{3,2,1,0:T(8,128)(2,1)S(1)} %get-tuple-element.556), channel_id=1, source_target_pairs={{0,8},{8,16},{16,24},{24,32},{32,40},{40,48},{48,56},{56,64},{64,7... | collective-permute-start | bytes 393224 | tf_op jit(solution)/shard_map/while/body/eval_jaxpr/ppermute | solution.py:17
  118.2 10.2 %collective-permute-start = (bf16[2,2,128,128]{3,2,1,0:T(8,128)(2,1)S(1)}, bf16[2,2,128,128]{3,2,1,0:T(8,128)(2,1)S(1)}, u32[]{:S(2)}, u32[]{:S(2)}) collective-permute-start(bf16[2,2,128,128]{3,2,1,0:T(8,128)(2,1)S(1)} %get-tuple-element.556), channel_id=1, source_target_pairs={{0,8},{8,16},{16,24},{24,32},{32,40},{40,48},{48,56},{56,64},{64,7... | collective-permute-start | bytes 393224 | tf_op jit(solution)/shard_map/while/body/eval_jaxpr/ppermute | solution.py:17
  128.4 10.2 %collective-permute-start = (bf16[2,2,128,128]{3,2,1,0:T(8,128)(2,1)S(1)}, bf16[2,2,128,128]{3,2,1,0:T(8,128)(2,1)S(1)}, u32[]{:S(2)}, u32[]{:S(2)}) collective-permute-start(bf16[2,2,128,128]{3,2,1,0:T(8,128)(2,1)S(1)} %get-tuple-element.556), channel_id=1, source_target_pairs={{0,8},{8,16},{16,24},{24,32},{32,40},{40,48},{48,56},{56,64},{64,7... | collective-permute-start | bytes 393224 | tf_op jit(solution)/shard_map/while/body/eval_jaxpr/ppermute | solution.py:17
  138.6 10.2 %collective-permute-start = (bf16[2,2,128,128]{3,2,1,0:T(8,128)(2,1)S(1)}, bf16[2,2,128,128]{3,2,1,0:T(8,128)(2,1)S(1)}, u32[]{:S(2)}, u32[]{:S(2)}) collective-permute-start(bf16[2,2,128,128]{3,2,1,0:T(8,128)(2,1)S(1)} %get-tuple-element.556), channel_id=1, source_target_pairs={{0,8},{8,16},{16,24},{24,32},{32,40},{40,48},{48,56},{56,64},{64,7... | collective-permute-start | bytes 393224 | tf_op jit(solution)/shard_map/while/body/eval_jaxpr/ppermute | solution.py:17
  148.8 10.2 %collective-permute-start = (bf16[2,2,128,128]{3,2,1,0:T(8,128)(2,1)S(1)}, bf16[2,2,128,128]{3,2,1,0:T(8,128)(2,1)S(1)}, u32[]{:S(2)}, u32[]{:S(2)}) collective-permute-start(bf16[2,2,128,128]{3,2,1,0:T(8,128)(2,1)S(1)} %get-tuple-element.556), channel_id=1, source_target_pairs={{0,8},{8,16},{16,24},{24,32},{32,40},{40,48},{48,56},{56,64},{64,7... | collective-permute-start | bytes 393224 | tf_op jit(solution)/shard_map/while/body/eval_jaxpr/ppermute | solution.py:17
  159.1 10.2 %collective-permute-start = (bf16[2,2,128,128]{3,2,1,0:T(8,128)(2,1)S(1)}, bf16[2,2,128,128]{3,2,1,0:T(8,128)(2,1)S(1)}, u32[]{:S(2)}, u32[]{:S(2)}) collective-permute-start(bf16[2,2,128,128]{3,2,1,0:T(8,128)(2,1)S(1)} %get-tuple-element.556), channel_id=1, source_target_pairs={{0,8},{8,16},{16,24},{24,32},{32,40},{40,48},{48,56},{56,64},{64,7... | collective-permute-start | bytes 393224 | tf_op jit(solution)/shard_map/while/body/eval_jaxpr/ppermute | solution.py:17
  169.3 10.2 %collective-permute-start = (bf16[2,2,128,128]{3,2,1,0:T(8,128)(2,1)S(1)}, bf16[2,2,128,128]{3,2,1,0:T(8,128)(2,1)S(1)}, u32[]{:S(2)}, u32[]{:S(2)}) collective-permute-start(bf16[2,2,128,128]{3,2,1,0:T(8,128)(2,1)S(1)} %get-tuple-element.556), channel_id=1, source_target_pairs={{0,8},{8,16},{16,24},{24,32},{32,40},{40,48},{48,56},{56,64},{64,7... | collective-permute-start | bytes 393224 | tf_op jit(solution)/shard_map/while/body/eval_jaxpr/ppermute | solution.py:17
  179.5 10.2 %collective-permute-start = (bf16[2,2,128,128]{3,2,1,0:T(8,128)(2,1)S(1)}, bf16[2,2,128,128]{3,2,1,0:T(8,128)(2,1)S(1)}, u32[]{:S(2)}, u32[]{:S(2)}) collective-permute-start(bf16[2,2,128,128]{3,2,1,0:T(8,128)(2,1)S(1)} %get-tuple-element.556), channel_id=1, source_target_pairs={{0,8},{8,16},{16,24},{24,32},{32,40},{40,48},{48,56},{56,64},{64,7... | collective-permute-start | bytes 393224 | tf_op jit(solution)/shard_map/while/body/eval_jaxpr/ppermute | solution.py:17
  189.7 10.2 %collective-permute-start = (bf16[2,2,128,128]{3,2,1,0:T(8,128)(2,1)S(1)}, bf16[2,2,128,128]{3,2,1,0:T(8,128)(2,1)S(1)}, u32[]{:S(2)}, u32[]{:S(2)}) collective-permute-start(bf16[2,2,128,128]{3,2,1,0:T(8,128)(2,1)S(1)} %get-tuple-element.556), channel_id=1, source_target_pairs={{0,8},{8,16},{16,24},{24,32},{32,40},{40,48},{48,56},{56,64},{64,7... | collective-permute-start | bytes 393224 | tf_op jit(solution)/shard_map/while/body/eval_jaxpr/ppermute | solution.py:17
  200.0 10.2 %collective-permute-start = (bf16[2,2,128,128]{3,2,1,0:T(8,128)(2,1)S(1)}, bf16[2,2,128,128]{3,2,1,0:T(8,128)(2,1)S(1)}, u32[]{:S(2)}, u32[]{:S(2)}) collective-permute-start(bf16[2,2,128,128]{3,2,1,0:T(8,128)(2,1)S(1)} %get-tuple-element.556), channel_id=1, source_target_pairs={{0,8},{8,16},{16,24},{24,32},{32,40},{40,48},{48,56},{56,64},{64,7... | collective-permute-start | bytes 393224 | tf_op jit(solution)/shard_map/while/body/eval_jaxpr/ppermute | solution.py:17
  210.2 10.2 %collective-permute-start = (bf16[2,2,128,128]{3,2,1,0:T(8,128)(2,1)S(1)}, bf16[2,2,128,128]{3,2,1,0:T(8,128)(2,1)S(1)}, u32[]{:S(2)}, u32[]{:S(2)}) collective-permute-start(bf16[2,2,128,128]{3,2,1,0:T(8,128)(2,1)S(1)} %get-tuple-element.556), channel_id=1, source_target_pairs={{0,8},{8,16},{16,24},{24,32},{32,40},{40,48},{48,56},{56,64},{64,7... | collective-permute-start | bytes 393224 | tf_op jit(solution)/shard_map/while/body/eval_jaxpr/ppermute | solution.py:17
  220.4 10.2 %collective-permute-start = (bf16[2,2,128,128]{3,2,1,0:T(8,128)(2,1)S(1)}, bf16[2,2,128,128]{3,2,1,0:T(8,128)(2,1)S(1)}, u32[]{:S(2)}, u32[]{:S(2)}) collective-permute-start(bf16[2,2,128,128]{3,2,1,0:T(8,128)(2,1)S(1)} %get-tuple-element.556), channel_id=1, source_target_pairs={{0,8},{8,16},{16,24},{24,32},{32,40},{40,48},{48,56},{56,64},{64,7... | collective-permute-start | bytes 393224 | tf_op jit(solution)/shard_map/while/body/eval_jaxpr/ppermute | solution.py:17
  230.7 10.2 %collective-permute-start = (bf16[2,2,128,128]{3,2,1,0:T(8,128)(2,1)S(1)}, bf16[2,2,128,128]{3,2,1,0:T(8,128)(2,1)S(1)}, u32[]{:S(2)}, u32[]{:S(2)}) collective-permute-start(bf16[2,2,128,128]{3,2,1,0:T(8,128)(2,1)S(1)} %get-tuple-element.556), channel_id=1, source_target_pairs={{0,8},{8,16},{16,24},{24,32},{32,40},{40,48},{48,56},{56,64},{64,7... | collective-permute-start | bytes 393224 | tf_op jit(solution)/shard_map/while/body/eval_jaxpr/ppermute | solution.py:17
  240.9 10.2 %collective-permute-start = (bf16[2,2,128,128]{3,2,1,0:T(8,128)(2,1)S(1)}, bf16[2,2,128,128]{3,2,1,0:T(8,128)(2,1)S(1)}, u32[]{:S(2)}, u32[]{:S(2)}) collective-permute-start(bf16[2,2,128,128]{3,2,1,0:T(8,128)(2,1)S(1)} %get-tuple-element.556), channel_id=1, source_target_pairs={{0,8},{8,16},{16,24},{24,32},{32,40},{40,48},{48,56},{56,64},{64,7... | collective-permute-start | bytes 393224 | tf_op jit(solution)/shard_map/while/body/eval_jaxpr/ppermute | solution.py:17
  251.1 10.2 %collective-permute-start = (bf16[2,2,128,128]{3,2,1,0:T(8,128)(2,1)S(1)}, bf16[2,2,128,128]{3,2,1,0:T(8,128)(2,1)S(1)}, u32[]{:S(2)}, u32[]{:S(2)}) collective-permute-start(bf16[2,2,128,128]{3,2,1,0:T(8,128)(2,1)S(1)} %get-tuple-element.556), channel_id=1, source_target_pairs={{0,8},{8,16},{16,24},{24,32},{32,40},{40,48},{48,56},{56,64},{64,7... | collective-permute-start | bytes 393224 | tf_op jit(solution)/shard_map/while/body/eval_jaxpr/ppermute | solution.py:17
  261.3 10.2 %collective-permute-start = (bf16[2,2,128,128]{3,2,1,0:T(8,128)(2,1)S(1)}, bf16[2,2,128,128]{3,2,1,0:T(8,128)(2,1)S(1)}, u32[]{:S(2)}, u32[]{:S(2)}) collective-permute-start(bf16[2,2,128,128]{3,2,1,0:T(8,128)(2,1)S(1)} %get-tuple-element.556), channel_id=1, source_target_pairs={{0,8},{8,16},{16,24},{24,32},{32,40},{40,48},{48,56},{56,64},{64,7... | collective-permute-start | bytes 393224 | tf_op jit(solution)/shard_map/while/body/eval_jaxpr/ppermute | solution.py:17
  271.6 10.2 %collective-permute-start = (bf16[2,2,128,128]{3,2,1,0:T(8,128)(2,1)S(1)}, bf16[2,2,128,128]{3,2,1,0:T(8,128)(2,1)S(1)}, u32[]{:S(2)}, u32[]{:S(2)}) collective-permute-start(bf16[2,2,128,128]{3,2,1,0:T(8,128)(2,1)S(1)} %get-tuple-element.556), channel_id=1, source_target_pairs={{0,8},{8,16},{16,24},{24,32},{32,40},{40,48},{48,56},{56,64},{64,7... | collective-permute-start | bytes 393224 | tf_op jit(solution)/shard_map/while/body/eval_jaxpr/ppermute | solution.py:17
  281.8 10.2 %collective-permute-start = (bf16[2,2,128,128]{3,2,1,0:T(8,128)(2,1)S(1)}, bf16[2,2,128,128]{3,2,1,0:T(8,128)(2,1)S(1)}, u32[]{:S(2)}, u32[]{:S(2)}) collective-permute-start(bf16[2,2,128,128]{3,2,1,0:T(8,128)(2,1)S(1)} %get-tuple-element.556), channel_id=1, source_target_pairs={{0,8},{8,16},{16,24},{24,32},{32,40},{40,48},{48,56},{56,64},{64,7... | collective-permute-start | bytes 393224 | tf_op jit(solution)/shard_map/while/body/eval_jaxpr/ppermute | solution.py:17
  292.0 10.2 %collective-permute-start = (bf16[2,2,128,128]{3,2,1,0:T(8,128)(2,1)S(1)}, bf16[2,2,128,128]{3,2,1,0:T(8,128)(2,1)S(1)}, u32[]{:S(2)}, u32[]{:S(2)}) collective-permute-start(bf16[2,2,128,128]{3,2,1,0:T(8,128)(2,1)S(1)} %get-tuple-element.556), channel_id=1, source_target_pairs={{0,8},{8,16},{16,24},{24,32},{32,40},{40,48},{48,56},{56,64},{64,7... | collective-permute-start | bytes 393224 | tf_op jit(solution)/shard_map/while/body/eval_jaxpr/ppermute | solution.py:17
  302.2 10.2 %collective-permute-start = (bf16[2,2,128,128]{3,2,1,0:T(8,128)(2,1)S(1)}, bf16[2,2,128,128]{3,2,1,0:T(8,128)(2,1)S(1)}, u32[]{:S(2)}, u32[]{:S(2)}) collective-permute-start(bf16[2,2,128,128]{3,2,1,0:T(8,128)(2,1)S(1)} %get-tuple-element.556), channel_id=1, source_target_pairs={{0,8},{8,16},{16,24},{24,32},{32,40},{40,48},{48,56},{56,64},{64,7... | collective-permute-start | bytes 393224 | tf_op jit(solution)/shard_map/while/body/eval_jaxpr/ppermute | solution.py:17
  312.5 10.2 %collective-permute-start = (bf16[2,2,128,128]{3,2,1,0:T(8,128)(2,1)S(1)}, bf16[2,2,128,128]{3,2,1,0:T(8,128)(2,1)S(1)}, u32[]{:S(2)}, u32[]{:S(2)}) collective-permute-start(bf16[2,2,128,128]{3,2,1,0:T(8,128)(2,1)S(1)} %get-tuple-element.556), channel_id=1, source_target_pairs={{0,8},{8,16},{16,24},{24,32},{32,40},{40,48},{48,56},{56,64},{64,7... | collective-permute-start | bytes 393224 | tf_op jit(solution)/shard_map/while/body/eval_jaxpr/ppermute | solution.py:17
  322.7 10.2 %collective-permute-start = (bf16[2,2,128,128]{3,2,1,0:T(8,128)(2,1)S(1)}, bf16[2,2,128,128]{3,2,1,0:T(8,128)(2,1)S(1)}, u32[]{:S(2)}, u32[]{:S(2)}) collective-permute-start(bf16[2,2,128,128]{3,2,1,0:T(8,128)(2,1)S(1)} %get-tuple-element.556), channel_id=1, source_target_pairs={{0,8},{8,16},{16,24},{24,32},{32,40},{40,48},{48,56},{56,64},{64,7... | collective-permute-start | bytes 393224 | tf_op jit(solution)/shard_map/while/body/eval_jaxpr/ppermute | solution.py:17
  332.9 10.2 %collective-permute-start = (bf16[2,2,128,128]{3,2,1,0:T(8,128)(2,1)S(1)}, bf16[2,2,128,128]{3,2,1,0:T(8,128)(2,1)S(1)}, u32[]{:S(2)}, u32[]{:S(2)}) collective-permute-start(bf16[2,2,128,128]{3,2,1,0:T(8,128)(2,1)S(1)} %get-tuple-element.556), channel_id=1, source_target_pairs={{0,8},{8,16},{16,24},{24,32},{32,40},{40,48},{48,56},{56,64},{64,7... | collective-permute-start | bytes 393224 | tf_op jit(solution)/shard_map/while/body/eval_jaxpr/ppermute | solution.py:17
  373.8 10.2 %collective-permute-start = (bf16[2,2,128,128]{3,2,1,0:T(8,128)(2,1)S(1)}, bf16[2,2,128,128]{3,2,1,0:T(8,128)(2,1)S(1)}, u32[]{:S(2)}, u32[]{:S(2)}) collective-permute-start(bf16[2,2,128,128]{3,2,1,0:T(8,128)(2,1)S(1)} %get-tuple-element.556), channel_id=1, source_target_pairs={{0,8},{8,16},{16,24},{24,32},{32,40},{40,48},{48,56},{56,64},{64,7... | collective-permute-start | bytes 393224 | tf_op jit(solution)/shard_map/while/body/eval_jaxpr/ppermute | solution.py:17
  384.1 10.2 %collective-permute-start = (bf16[2,2,128,128]{3,2,1,0:T(8,128)(2,1)S(1)}, bf16[2,2,128,128]{3,2,1,0:T(8,128)(2,1)S(1)}, u32[]{:S(2)}, u32[]{:S(2)}) collective-permute-start(bf16[2,2,128,128]{3,2,1,0:T(8,128)(2,1)S(1)} %get-tuple-element.556), channel_id=1, source_target_pairs={{0,8},{8,16},{16,24},{24,32},{32,40},{40,48},{48,56},{56,64},{64,7... | collective-permute-start | bytes 393224 | tf_op jit(solution)/shard_map/while/body/eval_jaxpr/ppermute | solution.py:17
  394.3 10.2 %collective-permute-start = (bf16[2,2,128,128]{3,2,1,0:T(8,128)(2,1)S(1)}, bf16[2,2,128,128]{3,2,1,0:T(8,128)(2,1)S(1)}, u32[]{:S(2)}, u32[]{:S(2)}) collective-permute-start(bf16[2,2,128,128]{3,2,1,0:T(8,128)(2,1)S(1)} %get-tuple-element.556), channel_id=1, source_target_pairs={{0,8},{8,16},{16,24},{24,32},{32,40},{40,48},{48,56},{56,64},{64,7... | collective-permute-start | bytes 393224 | tf_op jit(solution)/shard_map/while/body/eval_jaxpr/ppermute | solution.py:17
  404.5 10.2 %collective-permute-start = (bf16[2,2,128,128]{3,2,1,0:T(8,128)(2,1)S(1)}, bf16[2,2,128,128]{3,2,1,0:T(8,128)(2,1)S(1)}, u32[]{:S(2)}, u32[]{:S(2)}) collective-permute-start(bf16[2,2,128,128]{3,2,1,0:T(8,128)(2,1)S(1)} %get-tuple-element.556), channel_id=1, source_target_pairs={{0,8},{8,16},{16,24},{24,32},{32,40},{40,48},{48,56},{56,64},{64,7... | collective-permute-start | bytes 393224 | tf_op jit(solution)/shard_map/while/body/eval_jaxpr/ppermute | solution.py:17
  414.7 10.2 %collective-permute-start = (bf16[2,2,128,128]{3,2,1,0:T(8,128)(2,1)S(1)}, bf16[2,2,128,128]{3,2,1,0:T(8,128)(2,1)S(1)}, u32[]{:S(2)}, u32[]{:S(2)}) collective-permute-start(bf16[2,2,128,128]{3,2,1,0:T(8,128)(2,1)S(1)} %get-tuple-element.556), channel_id=1, source_target_pairs={{0,8},{8,16},{16,24},{24,32},{32,40},{40,48},{48,56},{56,64},{64,7... | collective-permute-start | bytes 393224 | tf_op jit(solution)/shard_map/while/body/eval_jaxpr/ppermute | solution.py:17
  476.1 10.2 %collective-permute-start = (bf16[2,2,128,128]{3,2,1,0:T(8,128)(2,1)S(1)}, bf16[2,2,128,128]{3,2,1,0:T(8,128)(2,1)S(1)}, u32[]{:S(2)}, u32[]{:S(2)}) collective-permute-start(bf16[2,2,128,128]{3,2,1,0:T(8,128)(2,1)S(1)} %get-tuple-element.556), channel_id=1, source_target_pairs={{0,8},{8,16},{16,24},{24,32},{32,40},{40,48},{48,56},{56,64},{64,7... | collective-permute-start | bytes 393224 | tf_op jit(solution)/shard_map/while/body/eval_jaxpr/ppermute | solution.py:17
  486.3 10.2 %collective-permute-start = (bf16[2,2,128,128]{3,2,1,0:T(8,128)(2,1)S(1)}, bf16[2,2,128,128]{3,2,1,0:T(8,128)(2,1)S(1)}, u32[]{:S(2)}, u32[]{:S(2)}) collective-permute-start(bf16[2,2,128,128]{3,2,1,0:T(8,128)(2,1)S(1)} %get-tuple-element.556), channel_id=1, source_target_pairs={{0,8},{8,16},{16,24},{24,32},{32,40},{40,48},{48,56},{56,64},{64,7... | collective-permute-start | bytes 393224 | tf_op jit(solution)/shard_map/while/body/eval_jaxpr/ppermute | solution.py:17
  496.5 10.2 %collective-permute-start = (bf16[2,2,128,128]{3,2,1,0:T(8,128)(2,1)S(1)}, bf16[2,2,128,128]{3,2,1,0:T(8,128)(2,1)S(1)}, u32[]{:S(2)}, u32[]{:S(2)}) collective-permute-start(bf16[2,2,128,128]{3,2,1,0:T(8,128)(2,1)S(1)} %get-tuple-element.556), channel_id=1, source_target_pairs={{0,8},{8,16},{16,24},{24,32},{32,40},{40,48},{48,56},{56,64},{64,7... | collective-permute-start | bytes 393224 | tf_op jit(solution)/shard_map/while/body/eval_jaxpr/ppermute | solution.py:17
  506.8 10.2 %collective-permute-start = (bf16[2,2,128,128]{3,2,1,0:T(8,128)(2,1)S(1)}, bf16[2,2,128,128]{3,2,1,0:T(8,128)(2,1)S(1)}, u32[]{:S(2)}, u32[]{:S(2)}) collective-permute-start(bf16[2,2,128,128]{3,2,1,0:T(8,128)(2,1)S(1)} %get-tuple-element.556), channel_id=1, source_target_pairs={{0,8},{8,16},{16,24},{24,32},{32,40},{40,48},{48,56},{56,64},{64,7... | collective-permute-start | bytes 393224 | tf_op jit(solution)/shard_map/while/body/eval_jaxpr/ppermute | solution.py:17
  517.0 10.2 %collective-permute-start = (bf16[2,2,128,128]{3,2,1,0:T(8,128)(2,1)S(1)}, bf16[2,2,128,128]{3,2,1,0:T(8,128)(2,1)S(1)}, u32[]{:S(2)}, u32[]{:S(2)}) collective-permute-start(bf16[2,2,128,128]{3,2,1,0:T(8,128)(2,1)S(1)} %get-tuple-element.556), channel_id=1, source_target_pairs={{0,8},{8,16},{16,24},{24,32},{32,40},{40,48},{48,56},{56,64},{64,7... | collective-permute-start | bytes 393224 | tf_op jit(solution)/shard_map/while/body/eval_jaxpr/ppermute | solution.py:17
  568.1 10.2 %collective-permute-start = (bf16[2,2,128,128]{3,2,1,0:T(8,128)(2,1)S(1)}, bf16[2,2,128,128]{3,2,1,0:T(8,128)(2,1)S(1)}, u32[]{:S(2)}, u32[]{:S(2)}) collective-permute-start(bf16[2,2,128,128]{3,2,1,0:T(8,128)(2,1)S(1)} %get-tuple-element.556), channel_id=1, source_target_pairs={{0,8},{8,16},{16,24},{24,32},{32,40},{40,48},{48,56},{56,64},{64,7... | collective-permute-start | bytes 393224 | tf_op jit(solution)/shard_map/while/body/eval_jaxpr/ppermute | solution.py:17
  578.4 10.2 %collective-permute-start = (bf16[2,2,128,128]{3,2,1,0:T(8,128)(2,1)S(1)}, bf16[2,2,128,128]{3,2,1,0:T(8,128)(2,1)S(1)}, u32[]{:S(2)}, u32[]{:S(2)}) collective-permute-start(bf16[2,2,128,128]{3,2,1,0:T(8,128)(2,1)S(1)} %get-tuple-element.556), channel_id=1, source_target_pairs={{0,8},{8,16},{16,24},{24,32},{32,40},{40,48},{48,56},{56,64},{64,7... | collective-permute-start | bytes 393224 | tf_op jit(solution)/shard_map/while/body/eval_jaxpr/ppermute | solution.py:17
  588.6 10.2 %collective-permute-start = (bf16[2,2,128,128]{3,2,1,0:T(8,128)(2,1)S(1)}, bf16[2,2,128,128]{3,2,1,0:T(8,128)(2,1)S(1)}, u32[]{:S(2)}, u32[]{:S(2)}) collective-permute-start(bf16[2,2,128,128]{3,2,1,0:T(8,128)(2,1)S(1)} %get-tuple-element.556), channel_id=1, source_target_pairs={{0,8},{8,16},{16,24},{24,32},{32,40},{40,48},{48,56},{56,64},{64,7... | collective-permute-start | bytes 393224 | tf_op jit(solution)/shard_map/while/body/eval_jaxpr/ppermute | solution.py:17
  598.8 10.2 %collective-permute-start = (bf16[2,2,128,128]{3,2,1,0:T(8,128)(2,1)S(1)}, bf16[2,2,128,128]{3,2,1,0:T(8,128)(2,1)S(1)}, u32[]{:S(2)}, u32[]{:S(2)}) collective-permute-start(bf16[2,2,128,128]{3,2,1,0:T(8,128)(2,1)S(1)} %get-tuple-element.556), channel_id=1, source_target_pairs={{0,8},{8,16},{16,24},{24,32},{32,40},{40,48},{48,56},{56,64},{64,7... | collective-permute-start | bytes 393224 | tf_op jit(solution)/shard_map/while/body/eval_jaxpr/ppermute | solution.py:17
  609.0 10.2 %collective-permute-start = (bf16[2,2,128,128]{3,2,1,0:T(8,128)(2,1)S(1)}, bf16[2,2,128,128]{3,2,1,0:T(8,128)(2,1)S(1)}, u32[]{:S(2)}, u32[]{:S(2)}) collective-permute-start(bf16[2,2,128,128]{3,2,1,0:T(8,128)(2,1)S(1)} %get-tuple-element.556), channel_id=1, source_target_pairs={{0,8},{8,16},{16,24},{24,32},{32,40},{40,48},{48,56},{56,64},{64,7... | collective-permute-start | bytes 393224 | tf_op jit(solution)/shard_map/while/body/eval_jaxpr/ppermute | solution.py:17
  (18 other events, 156.1 us)
where the time goes:
time: 691 us; the launch traced here: 688 us
  waiting for transfers between devices  437 us (63%)
  starting transfers between devices  121 us (18%)
  loops' own time  44.1 us (6%)
  other arithmetic  43 us (6%)
  blocking collectives  35.4 us (5%)
    ppermute x63, waiting for transfers between devices, from_behind(): return lax.ppermute(array, axis, pairs)  437 us
    ppermute x63, starting transfers between devices, from_behind(): return lax.ppermute(array, axis, pairs)  121 us
    another operation x1, loops' own time, per_device(): state = lax.fori_loop(1, steps + 1, turn, (blocks, state))[1]  44.1 us
    reduce_sum x64, other arithmetic, segment_ids(): jnp.sum((positions[:, None] >= doc_ends[None, :]).astype(jnp.int32), axis=1)  41.6 us
    psum x1, blocking collectives, per_device(): lse_gap = lax.psum(gap_part, 'tp') / QH  35.4 us
  transfers between devices with their start and end apart: 63, of which 63 were waited for; matrix products, arithmetic and copies ran while one was open for 6% of the time, Pallas kernels for 0%

commit v1 on v0

v1 whole, which is shorter than its diff:
```python
import functools

import jax
import jax.numpy as jnp
from jax import lax
from jax.experimental import pallas as pl
from jax.experimental.pallas import tpu as pltpu
from jax.sharding import PartitionSpec as P

QH = 64
KVH = 4
HD = 128
TOKENS = 8192
MOST = 4096
NDOCS = 16

ROWS_Y = 8
HALF_Y = 4
Z_LO = 4
CORES = 2
Z_HI = 2
TP = 8
BLOCK = 128
ROW_KEYS = Z_LO * CORES * BLOCK
HEADS = QH // TP
TILE = 256

LOG2E = 1.4426950408889634
LN2 = 0.6931471805599453
LOG2_SCALE = HD**-0.5 * LOG2E
MASKED = -1e30
MESH = pl.DeviceIdType.MESH


def kernel(
    q_hbm, k_hbm, v_hbm, doc_ref, out_hbm, lse_ref,
    kv, q_vm, o_vm, acc, peak, total, first, gaps,
    load_sem, out_sem, y_send, y_recv, z_send, z_recv, f_send, f_recv, s_send, s_recv, g_send, g_recv,
):
    ctx = lax.axis_index("ctx")
    tp = lax.axis_index("tp")
    y = ctx // (Z_LO * CORES)
    z_lo = (ctx // CORES) % Z_LO
    core = ctx % CORES
    x = tp // Z_HI
    z = (tp % Z_HI) * Z_LO + z_lo
    half = y // HALF_Y
    row = y % HALF_Y
    steps = 2 * (row + 1)

    def at_z(where):
        where = (where + 2 * Z_HI * Z_LO) % (Z_HI * Z_LO)
        return (y * (Z_LO * CORES) + (where % Z_LO) * CORES + core, x * Z_HI + where // Z_LO)

    def at_row(where):
        return ((half * HALF_Y + where) * (Z_LO * CORES) + z_lo * CORES + core, tp)

    above, below = at_z(z + 1), at_z(z - 1)
    sibling = (ctx + 1 - 2 * core, tp)
    z_next, z_prev, z_far = (z_lo + 1) % Z_LO, (z_lo + 3) % Z_LO, (z_lo + 2) % Z_LO

    head = pl.ds(pl.multiple_of(x * HD, HD), HD)
    loads = []
    for m in range(2):
        loads.append(pltpu.make_async_copy(k_hbm.at[m, :, head], kv.at[m, row, 0, z_lo, core], load_sem.at[m, 0]))
        loads.append(pltpu.make_async_copy(v_hbm.at[m, :, head], kv.at[m, row, 1, z_lo, core], load_sem.at[m, 1]))
    for m in range(2):
        loads.append(pltpu.make_async_copy(q_hbm.at[m], q_vm.at[m], load_sem.at[m, 2]))
    for load in loads:
        load.start()

    barrier = pltpu.get_barrier_semaphore()

    def greet(device):
        pl.semaphore_signal(barrier, inc=1, device_id=device, device_id_type=MESH)

    greet(above)
    greet(below)
    greet(sibling)
    for other in range(1, HALF_Y):
        greet(at_row((row + other) % HALF_Y))
    for other in range(1, TP):
        greet((ctx, (tp + other) % TP))

    position = ctx * BLOCK + lax.broadcasted_iota(jnp.int32, (BLOCK, 128), 0)
    begin = jnp.zeros((BLOCK, 128), jnp.int32)
    end = jnp.int32(0)
    for doc in range(NDOCS):
        end = end + doc_ref[doc]
        begin = jnp.where(position >= end, end, begin)
    first[...] = begin

    for load in loads[:4]:
        load.wait()
    pl.semaphore_wait(barrier, 3 + (HALF_Y - 1) + (TP - 1))

    def step_of(step):
        return step % 2, row - step // 2

    def remote(src, dst, send, recv, device):
        return pltpu.make_async_remote_copy(
            src_ref=src, dst_ref=dst, send_sem=send, recv_sem=recv, device_id=device, device_id_type=MESH
        )

    def up_copy(m, other):
        mine = kv.at[m, row, :, z_lo, core]
        return remote(mine, mine, y_send.at[m, other], y_recv.at[m, row], at_row(other))

    def from_row(m, r):
        block = kv.at[m, r, :, z_lo, core]
        return remote(block, block, y_send.at[m, 0], y_recv.at[m, r], at_row(r))

    def z_copy(m, r, way):
        block = kv.at[m, r, :, z_lo, core]
        return remote(block, block, z_send.at[m, r, way], z_recv.at[m, r, way], below if way else above)

    def z_arrival(m, r, way):
        block = kv.at[m, r, :, z_next if way else z_prev, core]
        return remote(block, block, z_send.at[m, r, way], z_recv.at[m, r, way], above if way else below)

    def far_copy(m, r, way):
        block = kv.at[m, r, way, z_next if way else z_prev, core]
        return remote(block, block, f_send.at[m, r, way], f_recv.at[m, r, way], below if way else above)

    def far_arrival(m, r, way):
        block = kv.at[m, r, way, z_far, core]
        return remote(block, block, f_send.at[m, r, way], f_recv.at[m, r, way], above if way else below)

    columns = (z_lo, z_prev, z_next, z_far)

    def sib_copy(m, r, kind):
        block = kv.at[m, r, :, columns[kind], core]
        return remote(block, block, s_send.at[m, r, kind], s_recv.at[m, r, kind], sibling)

    def sib_arrival(m, r, kind):
        block = kv.at[m, r, :, columns[kind], 1 - core]
        return remote(block, block, s_send.at[m, r, kind], s_recv.at[m, r, kind], sibling)

    def spread(step, own):
        m, r = step_of(step)
        if not own:
            from_row(m, r).wait_recv()
        z_copy(m, r, 0).start()
        z_copy(m, r, 1).start()
        sib_copy(m, r, 0).start()

    def relay(step):
        m, r = step_of(step)
        for way in range(2):
            z_arrival(m, r, way).wait_recv()
            far_copy(m, r, way).start()
            sib_copy(m, r, 1 + way).start()

    def finish(step):
        m, r = step_of(step)
        for way in range(2):
            far_arrival(m, r, way).wait_recv()
        sib_copy(m, r, 3).start()

    def gather_done(step):
        m, r = step_of(step)
        for kind in range(4):
            sib_arrival(m, r, kind).wait_recv()

    def attend(step, causal):
        m, r = step_of(step)
        key_base = (half * HALF_Y + r) * ROW_KEYS
        keys = kv[m, r, 0].reshape(ROW_KEYS, HD)
        values = kv[m, r, 1].reshape(ROW_KEYS, HD)
        values = jnp.concatenate([values, jnp.ones((ROW_KEYS, 128), jnp.bfloat16)], axis=1)
        low = first[...] - key_base
        low = jnp.concatenate([low] * (TILE // BLOCK), axis=0)[:, :1]
        key_at = lax.broadcasted_iota(jnp.int32, (TILE, ROW_KEYS), 1)
        for tile in range(HEADS * BLOCK // TILE):
            rows = pl.ds(tile * TILE, TILE)
            heads = range(tile * (TILE // BLOCK), (tile + 1) * (TILE // BLOCK))
            q = jnp.concatenate([q_vm[m, :, pl.ds(h * HD, HD)] for h in heads], axis=0)
            scores = lax.dot_general(q, keys, (((1,), (1,)), ((), ())), preferred_element_type=jnp.float32)
            visible = key_at >= low
            if causal:
                query_at = lax.broadcasted_iota(jnp.int32, (TILE, ROW_KEYS), 0) % BLOCK
                query_at = query_at + (z_lo * CORES + core) * BLOCK
                visible = visible & (key_at <= query_at)
            scores = jnp.where(visible, scores, MASKED)
            here = jnp.max(scores, axis=1, keepdims=True) * LOG2_SCALE
            if causal:
                top = jnp.broadcast_to(here, (TILE, 128))
            else:
                old = peak[m, rows, :]
                top = jnp.maximum(old, here)
                factor = jnp.exp2(old - top)
            weights = jnp.exp2(scores * LOG2_SCALE - top[:, :1]).astype(jnp.bfloat16)
            both = jnp.dot(weights, values, preferred_element_type=jnp.float32)
            if causal:
                acc[m, rows, :] = both[:, :HD]
                total[m, rows, :] = both[:, HD:]
            else:
                acc[m, rows, :] = acc[m, rows, :] * factor + both[:, :HD]
                total[m, rows, :] = total[m, rows, :] * factor + both[:, HD:]
            peak[m, rows, :] = top

    def when_live(step, act):
        @pl.when(step < steps)
        def _():
            act(step)

    spread(0, True)
    for other in range(1, HALF_Y):
        @pl.when(other > row)
        def _():
            up_copy(0, other).start()
    spread(1, True)
    for other in range(1, HALF_Y):
        @pl.when(other > row)
        def _():
            up_copy(1, other).start()
    relay(0)
    when_live(2, lambda step: spread(step, False))
    relay(1)
    finish(0)
    for load in loads[4:]:
        load.wait()

    def slot(step, causal):
        gather_done(step)
        when_live(step + 1, finish)
        when_live(step + 2, relay)
        when_live(step + 3, lambda later: spread(later, False))
        attend(step, causal)
        return 0

    lax.fori_loop(0, 2, lambda step, _: slot(step, True), 0)
    lax.fori_loop(2, steps, lambda step, _: slot(step, False), 0)

    gap = jnp.zeros((BLOCK, 128), jnp.float32)
    for h in range(HEADS):
        rows = pl.ds(h * BLOCK, BLOCK)
        gap = gap + ((peak[0, rows, :] - peak[1, rows, :]) * LN2 + (jnp.log(total[0, rows, :]) - jnp.log(total[1, rows, :])))
    gaps[tp] = gap.T[:8, :]

    def gap_copy(other):
        return remote(gaps.at[tp], gaps.at[tp], g_send.at[other], g_recv.at[tp], (ctx, (tp + other) % TP))

    def gap_arrival(other):
        peer = (tp + other) % TP
        return remote(gaps.at[peer], gaps.at[peer], g_send.at[other], g_recv.at[peer], (ctx, peer))

    for other in range(1, TP):
        gap_copy(other).start()

    stores = []
    for m in range(2):
        for h in range(HEADS):
            rows = pl.ds(h * BLOCK, BLOCK)
            o_vm[m, :, pl.ds(h * HD, HD)] = (acc[m, rows, :] / total[m, rows, :]).astype(jnp.bfloat16)
        stores.append(pltpu.make_async_copy(o_vm.at[m], out_hbm.at[m], out_sem.at[m]))
        stores[m].start()

    def wait_sends(step, _):
        m, r = step_of(step)
        for way in range(2):
            z_copy(m, r, way).wait_send()
            far_copy(m, r, way).wait_send()
        for kind in range(4):
            sib_copy(m, r, kind).wait_send()
        return 0

    lax.fori_loop(0, steps, wait_sends, 0)
    for m in range(2):
        for other in range(1, HALF_Y):
            @pl.when(other > row)
            def _():
                up_copy(m, other).wait_send()

    for other in range(1, TP):
        gap_arrival(other).wait_recv()
    whole = gaps[0]
    for peer in range(1, TP):
        whole = whole + gaps[peer]
    lse_ref[...] = whole[:1, :] * (1.0 / QH)
    for other in range(1, TP):
        gap_copy(other).wait_send()
    for store in stores:
        store.wait()


def per_device(queries, keys, values, doc_lengths):
    dma = pltpu.SemaphoreType.DMA
    attended, gap = pl.pallas_call(
        kernel,
        out_shape=[
            jax.ShapeDtypeStruct((2, BLOCK, HEADS * HD), jnp.bfloat16),
            jax.ShapeDtypeStruct((1, BLOCK), jnp.float32),
        ],
        in_specs=[pl.BlockSpec(memory_space=pl.ANY)] * 3 + [pl.BlockSpec(memory_space=pltpu.SMEM)],
        out_specs=[pl.BlockSpec(memory_space=pl.ANY), pl.BlockSpec(memory_space=pltpu.VMEM)],
        scratch_shapes=[
            pltpu.VMEM((2, HALF_Y, 2, Z_LO, CORES, BLOCK, HD), jnp.bfloat16),
            pltpu.VMEM((2, BLOCK, HEADS * HD), jnp.bfloat16),
            pltpu.VMEM((2, BLOCK, HEADS * HD), jnp.bfloat16),
            pltpu.VMEM((2, HEADS * BLOCK, HD), jnp.float32),
            pltpu.VMEM((2, HEADS * BLOCK, 128), jnp.float32),
            pltpu.VMEM((2, HEADS * BLOCK, 128), jnp.float32),
            pltpu.VMEM((BLOCK, 128), jnp.int32),
            pltpu.VMEM((TP, 8, 128), jnp.float32),
            dma((2, 3)),
            dma((2,)),
            dma((2, HALF_Y)),
            dma((2, HALF_Y)),
            dma((2, HALF_Y, 2)),
            dma((2, HALF_Y, 2)),
            dma((2, HALF_Y, 2)),
            dma((2, HALF_Y, 2)),
            dma((2, HALF_Y, 4)),
            dma((2, HALF_Y, 4)),
            dma((TP,)),
            dma((TP,)),
        ],
        compiler_params=pltpu.CompilerParams(
            collective_id=0, has_side_effects=True, vmem_limit_bytes=48 * 2**20
        ),
        name="packed_attention",
    )(queries, keys, values, doc_lengths)
    return attended, gap.reshape(BLOCK)


def solution(mesh):
    in_specs = (P(None, "ctx", "tp"), P(None, "ctx", None), P(None, "ctx", None), P())
    out_specs = (P(None, "ctx", "tp"), P("ctx"))
    return jax.shard_map(
        per_device, mesh=mesh, in_specs=in_specs, out_specs=out_specs, check_vma=False
    )
```

time: 691 us -> 64.8 us (0.09)
  the two profiles are of different devices: /device:TPU:32 before, /device:TPU:56 now
where the time goes in v1:
time: 64.8 us; the launch traced here: 64.4 us
  Pallas kernels  58.9 us (91%)
  local copies, waits for them, and re-layouts  4.9 us (8%)
  between operations  0.65 us (1%)
    pallas_call x1, Pallas kernels, per_device(): pl.pallas_call(kernel, out_shape=[jax.ShapeDtypeStruct((2, BLOCK, HEADS *...  58.9 us
    unnamed x10, local copies, waits for them, and re-layouts  4.9 us

profile of v1, /device:TPU:56, one launch (start us, length us, event | category | flops | bytes accessed | tf_op | source)
XLA Modules:
  0.0 64.4 jit_solution(15348391477248739167)
XLA Ops:
  0.6 0.0 copy-start
  0.6 1.0 %copy-done = bf16[2,128,1024]{2,1,0:T(8,128)(2,1)S(1)} copy-done((bf16[2,128,1024]{2,1,0:T(8,128)(2,1)S(1)}, bf16[2,128,1024]{2,1,0:T(8,128)(2,1)}, u32[]{:S(2)}) %copy-start) | copy-done | bytes 524312
  1.7 0.0 copy-start.1
  1.7 0.9 %copy-done.1 = bf16[2,128,512]{2,1,0:T(8,128)(2,1)S(1)} copy-done((bf16[2,128,512]{2,1,0:T(8,128)(2,1)S(1)}, bf16[2,128,512]{2,1,0:T(8,128)(2,1)}, u32[]{:S(2)}) %copy-start.1) | copy-done | bytes 262168
  2.6 0.0 copy-start.2
  2.6 0.9 %copy-done.2 = bf16[2,128,512]{2,1,0:T(8,128)(2,1)S(1)} copy-done((bf16[2,128,512]{2,1,0:T(8,128)(2,1)S(1)}, bf16[2,128,512]{2,1,0:T(8,128)(2,1)}, u32[]{:S(2)}) %copy-start.2) | copy-done | bytes 262168
  3.6 0.0 copy-start.3
  3.6 0.7 %copy-done.3 = s32[16]{0:T(128)S(1)} copy-done((s32[16]{0:T(128)S(1)}, s32[16]{0:T(128)}, u32[]{:S(2)}) %copy-start.3) | copy-done | bytes 88
  4.2 58.9 %packed_attention.1 = (bf16[2,128,1024]{2,1,0:T(8,128)(2,1)S(1)}, f32[1,128]{1,0:T(1,128)S(1)}) custom-call(bf16[2,128,1024]{2,1,0:T(8,128)(2,1)S(1)} %copy-done, bf16[2,128,512]{2,1,0:T(8,128)(2,1)S(1)} %copy-done.1, bf16[2,128,512]{2,1,0:T(8,128)(2,1)S(1)} %copy-done.2, s32[16]{0:T(128)S(1)} %copy-done.3), custom_call_target="tpu_custom_call" | custom-call | tf_op jit(solution)/shard_map/packed_attention/pallas_call | solution.py:289
  63.1 0.8 %copy.8 = bf16[2,128,1024]{2,1,0:T(8,128)(2,1)} copy(bf16[2,128,1024]{2,1,0:T(8,128)(2,1)S(1)} %get-tuple-element.8) | data formatting | bytes 1048576
  63.9 0.5 copy.9
Async XLA Ops:
  0.6 1.0 %copy-start = (bf16[2,128,1024]{2,1,0:T(8,128)(2,1)S(1)}, bf16[2,128,1024]{2,1,0:T(8,128)(2,1)}, u32[]{:S(2)}) copy-start(bf16[2,128,1024]{2,1,0:T(8,128)(2,1)} %q_hbm.1) | copy-start | bytes 1572868
  1.7 0.9 %copy-start.1 = (bf16[2,128,512]{2,1,0:T(8,128)(2,1)S(1)}, bf16[2,128,512]{2,1,0:T(8,128)(2,1)}, u32[]{:S(2)}) copy-start(bf16[2,128,512]{2,1,0:T(8,128)(2,1)} %k_hbm.1) | copy-start | bytes 786436
  2.6 0.9 %copy-start.2 = (bf16[2,128,512]{2,1,0:T(8,128)(2,1)S(1)}, bf16[2,128,512]{2,1,0:T(8,128)(2,1)}, u32[]{:S(2)}) copy-start(bf16[2,128,512]{2,1,0:T(8,128)(2,1)} %v_hbm.1) | copy-start | bytes 786436
  3.6 0.7 %copy-start.3 = (s32[16]{0:T(128)S(1)}, s32[16]{0:T(128)}, u32[]{:S(2)}) copy-start(s32[16]{0:T(128)} %doc_ref.1) | copy-start | bytes 196

commit v2 on v1

--- a/solution.py
+++ b/solution.py
@@ -29,13 +29,28 @@
 LN2 = 0.6931471805599453
 LOG2_SCALE = HD**-0.5 * LOG2E
 MASKED = -1e30
+EMPTY = -1e35
 MESH = pl.DeviceIdType.MESH
+
+
+AHEAD = {
+    0: (("relay", 1),),
+    1: (("finish", 1), ("spread", 4)),
+    2: (("relay", 2), ("spread", 5)),
+    3: (("finish", 2),),
+    4: (("relay", 3), ("spread", 6)),
+    5: (("finish", 3), ("spread", 7)),
+    7: (("relay", 4), ("finish", 4)),
+    9: (("relay", 5), ("finish", 5)),
+    11: (("relay", 6), ("finish", 6)),
+    13: (("relay", 7), ("finish", 7)),
+}
 
 
 def kernel(
     q_hbm, k_hbm, v_hbm, doc_ref, out_hbm, lse_ref,
-    kv, q_vm, o_vm, acc, peak, total, first, gaps,
-    load_sem, out_sem, y_send, y_recv, z_send, z_recv, f_send, f_recv, s_send, s_recv, g_send, g_recv,
+    kv, q_vm, o_vm, acc, peak, total, bias, eye, scores_0, scores_1, weights_0, weights_1, factor_0, factor_1, gaps,
+    load_sem, out_sem, y_send, y_recv, z_send, z_recv, f_send, f_recv, s_send, s_recv, u_send, u_recv, g_send, g_recv,
 ):
     ctx = lax.axis_index("ctx")
     tp = lax.axis_index("tp")
@@ -76,23 +91,36 @@
 
     greet(above)
     greet(below)
+    greet(at_z(z + 2))
+    greet(at_z(z - 2))
     greet(sibling)
     for other in range(1, HALF_Y):
         greet(at_row((row + other) % HALF_Y))
     for other in range(1, TP):
         greet((ctx, (tp + other) % TP))
 
-    position = ctx * BLOCK + lax.broadcasted_iota(jnp.int32, (BLOCK, 128), 0)
-    begin = jnp.zeros((BLOCK, 128), jnp.int32)
+    position = ctx * BLOCK + lax.broadcasted_iota(jnp.int32, (8, BLOCK), 1)
+    begin = jnp.zeros((8, BLOCK), jnp.int32)
     end = jnp.int32(0)
     for doc in range(NDOCS):
         end = end + doc_ref[doc]
         begin = jnp.where(position >= end, end, begin)
-    first[...] = begin
+
+    acc[...] = jnp.zeros_like(acc)
+    total[...] = jnp.zeros_like(total)
+    peak[...] = jnp.full_like(peak, MASKED)
+    scores_1[...] = jnp.full_like(scores_1, EMPTY)
+    for ref in (weights_0, weights_1):
+        ref[...] = jnp.zeros_like(ref)
+    for ref in (factor_0, factor_1):
+        ref[...] = jnp.ones_like(ref)
+    eye[...] = (
+        lax.broadcasted_iota(jnp.int32, (BLOCK, BLOCK), 0) == lax.broadcasted_iota(jnp.int32, (BLOCK, BLOCK), 1)
+    ).astype(jnp.bfloat16)
 
     for load in loads[:4]:
         load.wait()
-    pl.semaphore_wait(barrier, 3 + (HALF_Y - 1) + (TP - 1))
+    pl.semaphore_wait(barrier, 5 + (HALF_Y - 1) + (TP - 1))
 
     def step_of(step):
         return step % 2, row - step // 2
@@ -119,12 +147,23 @@
         return remote(block, block, z_send.at[m, r, way], z_recv.at[m, r, way], above if way else below)
 
     def far_copy(m, r, way):
-        block = kv.at[m, r, way, z_next if way else z_prev, core]
-        return remote(block, block, f_send.at[m, r, way], f_recv.at[m, r, way], below if way else above)
+        block = kv.at[m, r, way, z_lo, core]
+        return remote(block, block, f_send.at[m, r, way], f_recv.at[m, r, way], at_z(z - 2 if way else z + 2))
 
     def far_arrival(m, r, way):
         block = kv.at[m, r, way, z_far, core]
-        return remote(block, block, f_send.at[m, r, way], f_recv.at[m, r, way], above if way else below)
+        return remote(block, block, f_send.at[m, r, way], f_recv.at[m, r, way], at_z(z + 2 if way else z - 2))
+
+    def far_up(m):
+        block = kv.at[m, row, :, z_far, core]
+        return remote(block, block, u_send.at[m], u_recv.at[m, row], at_row(HALF_Y - 1))
+
+    def far_from_row(m, r):
+        block = kv.at[m, r, :, z_far, core]
+        return remote(block, block, u_send.at[m], u_recv.at[m, r], at_row(r))
+
+    top_row = row == HALF_Y - 1
+    sends_far_up = row < HALF_Y - 2
 
     columns = (z_lo, z_prev, z_next, z_far)
 
@@ -136,101 +175,148 @@
         block = kv.at[m, r, :, columns[kind], 1 - core]
         return remote(block, block, s_send.at[m, r, kind], s_recv.at[m, r, kind], sibling)
 
-    def spread(step, own):
+    def pass_on(m, r):
+        for way in range(2):
+            z_copy(m, r, way).start()
+        sib_copy(m, r, 0).start()
+
+    def far_by_z(step):
+        return jnp.logical_not(top_row & (step >= 4))
+
+    def spread(step):
         m, r = step_of(step)
-        if not own:
-            from_row(m, r).wait_recv()
-        z_copy(m, r, 0).start()
-        z_copy(m, r, 1).start()
-        sib_copy(m, r, 0).start()
+        from_row(m, r).wait_recv()
+        pass_on(m, r)
+
+        @pl.when(far_by_z(step))
+        def _():
+            for way in range(2):
+                far_copy(m, r, way).start()
 
     def relay(step):
         m, r = step_of(step)
         for way in range(2):
             z_arrival(m, r, way).wait_recv()
-            far_copy(m, r, way).start()
             sib_copy(m, r, 1 + way).start()
 
     def finish(step):
         m, r = step_of(step)
-        for way in range(2):
-            far_arrival(m, r, way).wait_recv()
+
+        @pl.when(far_by_z(step))
+        def _():
+            for way in range(2):
+                far_arrival(m, r, way).wait_recv()
+
+        @pl.when(jnp.logical_not(far_by_z(step)))
+        def _():
+            far_from_row(m, r).wait_recv()
+
         sib_copy(m, r, 3).start()
+
+        @pl.when(sends_far_up & (step < 2))
+        def _():
+            far_up(m).start()
 
     def gather_done(step):
         m, r = step_of(step)
         for kind in range(4):
             sib_arrival(m, r, kind).wait_recv()
 
-    def attend(step, causal):
-        m, r = step_of(step)
-        key_base = (half * HALF_Y + r) * ROW_KEYS
-        keys = kv[m, r, 0].reshape(ROW_KEYS, HD)
-        values = kv[m, r, 1].reshape(ROW_KEYS, HD)
-        values = jnp.concatenate([values, jnp.ones((ROW_KEYS, 128), jnp.bfloat16)], axis=1)
-        low = first[...] - key_base
-        low = jnp.concatenate([low] * (TILE // BLOCK), axis=0)[:, :1]
-        key_at = lax.broadcasted_iota(jnp.int32, (TILE, ROW_KEYS), 1)
-        for tile in range(HEADS * BLOCK // TILE):
-            rows = pl.ds(tile * TILE, TILE)
-            heads = range(tile * (TILE // BLOCK), (tile + 1) * (TILE // BLOCK))
-            q = jnp.concatenate([q_vm[m, :, pl.ds(h * HD, HD)] for h in heads], axis=0)
-            scores = lax.dot_general(q, keys, (((1,), (1,)), ((), ())), preferred_element_type=jnp.float32)
-            visible = key_at >= low
-            if causal:
-                query_at = lax.broadcasted_iota(jnp.int32, (TILE, ROW_KEYS), 0) % BLOCK
-                query_at = query_at + (z_lo * CORES + core) * BLOCK
-                visible = visible & (key_at <= query_at)
-            scores = jnp.where(visible, scores, MASKED)
-            here = jnp.max(scores, axis=1, keepdims=True) * LOG2_SCALE
-            if causal:
-                top = jnp.broadcast_to(here, (TILE, 128))
-            else:
-                old = peak[m, rows, :]
-                top = jnp.maximum(old, here)
-                factor = jnp.exp2(old - top)
-            weights = jnp.exp2(scores * LOG2_SCALE - top[:, :1]).astype(jnp.bfloat16)
-            both = jnp.dot(weights, values, preferred_element_type=jnp.float32)
-            if causal:
-                acc[m, rows, :] = both[:, :HD]
-                total[m, rows, :] = both[:, HD:]
-            else:
-                acc[m, rows, :] = acc[m, rows, :] * factor + both[:, :HD]
-                total[m, rows, :] = total[m, rows, :] * factor + both[:, HD:]
-            peak[m, rows, :] = top
+    pairs = HEADS * BLOCK // TILE // 2
+    tile_heads = TILE // BLOCK
+    scores, weights, factors = (scores_0, scores_1), (weights_0, weights_1), (factor_0, factor_1)
+
+    def place(tile):
+        tile = jnp.maximum(tile, 0)
+        m, r = step_of(tile // (2 * pairs))
+        return m, r, tile % (2 * pairs)
+
+    def score(tile, slot):
+        m, r, at = place(tile)
+        heads = [
+            q_vm[m, :, pl.ds(pl.multiple_of((at * tile_heads + h) * HD, HD), HD)] for h in range(tile_heads)
+        ]
+        q = jnp.concatenate([jnp.concatenate([h, eye[...]], axis=1) for h in heads], axis=0)
+        keys = jnp.concatenate([kv[m, r, 0].reshape(ROW_KEYS, HD), bias[r]], axis=1)
+        scores[slot][...] = lax.dot_general(q, keys, (((1,), (1,)), ((), ())), preferred_element_type=jnp.float32)
+
+    def weigh(tile, slot):
+        m, r, at = place(tile)
+        rows = pl.ds(pl.multiple_of(at * TILE, TILE), TILE)
+        here = scores[slot][...]
+        old = peak[m, rows, :]
+        new = jnp.maximum(old, jnp.max(here, axis=1, keepdims=True) * LOG2_SCALE)
+        factors[slot][...] = jnp.exp2(old - new)
+        peak[m, rows, :] = new
+        weights[slot][...] = jnp.exp2(here * LOG2_SCALE - new[:, :1]).astype(jnp.bfloat16)
+
+    def gather(tile, slot):
+        m, r, at = place(tile)
+        rows = pl.ds(pl.multiple_of(at * TILE, TILE), TILE)
+        values = jnp.concatenate([kv[m, r, 1].reshape(ROW_KEYS, HD), jnp.ones((ROW_KEYS, 128), jnp.bfloat16)], axis=1)
+        both = jnp.dot(weights[slot][...], values, preferred_element_type=jnp.float32)
+        acc[m, rows, :] = acc[m, rows, :] * factors[slot][...] + both[:, :HD]
+        total[m, rows, :] = total[m, rows, :] * factors[slot][...] + both[:, HD:]
+
+    def mask_row(r, _):
+        key_at = (half * HALF_Y + r) * ROW_KEYS + lax.broadcasted_iota(jnp.int32, (ROW_KEYS, BLOCK), 0)
+        visible = (key_at >= begin[:1, :]) & (key_at <= position[:1, :])
+        bias[r] = jnp.where(visible, 0.0, MASKED).astype(jnp.bfloat16)
+        return 0
 
     def when_live(step, act):
         @pl.when(step < steps)
         def _():
             act(step)
 
-    spread(0, True)
-    for other in range(1, HALF_Y):
-        @pl.when(other > row)
-        def _():
-            up_copy(0, other).start()
-    spread(1, True)
-    for other in range(1, HALF_Y):
-        @pl.when(other > row)
-        def _():
-            up_copy(1, other).start()
+    def up(other):
+        @pl.when(other < HALF_Y)
+        def _():
+            for m in range(2):
+                up_copy(m, other).start()
+
+    for m in range(2):
+        pass_on(m, row)
+        for way in range(2):
+            far_copy(m, row, way).start()
+    up(row + 1)
+    lax.fori_loop(0, row + 1, mask_row, 0)
     relay(0)
-    when_live(2, lambda step: spread(step, False))
-    relay(1)
+    for other in (3, 2):
+        @pl.when(other > row + 1)
+        def _():
+            up(other)
+    when_live(2, spread)
     finish(0)
+    when_live(3, spread)
     for load in loads[4:]:
         load.wait()
 
-    def slot(step, causal):
-        gather_done(step)
-        when_live(step + 1, finish)
-        when_live(step + 2, relay)
-        when_live(step + 3, lambda later: spread(later, False))
-        attend(step, causal)
+    def pair(at, _):
+        for here, acts in AHEAD.items():
+            @pl.when(at == here)
+            def _():
+                for act, step in acts:
+                    when_live(step, {"spread": spread, "relay": relay, "finish": finish}[act])
+
+        @pl.when(at % pairs == 0)
+        def _():
+            gather_done(at // pairs)
+
+        tile = 2 * at
+        score(tile, 0)
+        weigh(tile - 1, 1)
+        gather(tile - 2, 0)
+        score(tile + 1, 1)
+        weigh(tile, 0)
+        gather(tile - 1, 1)
         return 0
 
-    lax.fori_loop(0, 2, lambda step, _: slot(step, True), 0)
-    lax.fori_loop(2, steps, lambda step, _: slot(step, False), 0)
+    lax.fori_loop(0, pairs * steps, pair, 0)
+    tiles = 2 * pairs * steps
+    weigh(tiles - 1, 1)
+    gather(tiles - 2, 0)
+    gather(tiles - 1, 1)
 
     gap = jnp.zeros((BLOCK, 128), jnp.float32)
     for h in range(HEADS):
@@ -260,7 +346,12 @@
         m, r = step_of(step)
         for way in range(2):
             z_copy(m, r, way).wait_send()
-            far_copy(m, r, way).wait_send()
+
+        @pl.when(far_by_z(step))
+        def _():
+            for way in range(2):
+                far_copy(m, r, way).wait_send()
+
         for kind in range(4):
             sib_copy(m, r, kind).wait_send()
         return 0
@@ -271,6 +362,10 @@
             @pl.when(other > row)
             def _():
                 up_copy(m, other).wait_send()
+
+        @pl.when(sends_far_up)
+        def _():
+            far_up(m).wait_send()
 
     for other in range(1, TP):
         gap_arrival(other).wait_recv()
@@ -301,7 +396,14 @@
             pltpu.VMEM((2, HEADS * BLOCK, HD), jnp.float32),
             pltpu.VMEM((2, HEADS * BLOCK, 128), jnp.float32),
             pltpu.VMEM((2, HEADS * BLOCK, 128), jnp.float32),
-            pltpu.VMEM((BLOCK, 128), jnp.int32),
+            pltpu.VMEM((HALF_Y, ROW_KEYS, BLOCK), jnp.bfloat16),
+            pltpu.VMEM((BLOCK, BLOCK), jnp.bfloat16),
+            pltpu.VMEM((TILE, ROW_KEYS), jnp.float32),
+            pltpu.VMEM((TILE, ROW_KEYS), jnp.float32),
+            pltpu.VMEM((TILE, ROW_KEYS), jnp.bfloat16),
+            pltpu.VMEM((TILE, ROW_KEYS), jnp.bfloat16),
+            pltpu.VMEM((TILE, 128), jnp.float32),
+            pltpu.VMEM((TILE, 128), jnp.float32),
             pltpu.VMEM((TP, 8, 128), jnp.float32),
             dma((2, 3)),
             dma((2,)),
@@ -313,11 +415,13 @@
             dma((2, HALF_Y, 2)),
             dma((2, HALF_Y, 4)),
             dma((2, HALF_Y, 4)),
+            dma((2,)),
+            dma((2, HALF_Y)),
             dma((TP,)),
             dma((TP,)),
         ],
         compiler_params=pltpu.CompilerParams(
-            collective_id=0, has_side_effects=True, vmem_limit_bytes=48 * 2**20
+            collective_id=0, has_side_effects=True, vmem_limit_bytes=60 * 2**20
         ),
         name="packed_attention",
     )(queries, keys, values, doc_lengths)

time: 64.8 us -> 57.1 us (0.88)
  Pallas kernels: 58.9 us -> 53.9 us
  local copies, waits for them, and re-layouts: 4.9 us -> 2.38 us
    pallas_call x1, Pallas kernels: 58.9 us -> 53.9 us  [per_device(): pl.pallas_call(kernel, out_shape=[jax.ShapeDtypeStruct((2, BLOCK, HEADS *...]
    unnamed x10 -> x4, local copies, waits for them, and re-layouts: 4.9 us -> 2.38 us
where the time goes in v2:
time: 57.1 us; the launch traced here: 57 us
  Pallas kernels  53.9 us (94%)
  local copies, waits for them, and re-layouts  2.38 us (4%)
  between operations  0.65 us (1%)
    pallas_call x1, Pallas kernels, per_device(): pl.pallas_call(kernel, out_shape=[jax.ShapeDtypeStruct((2, BLOCK, HEADS *...  53.9 us
    unnamed x4, local copies, waits for them, and re-layouts  2.38 us

profile of v2, /device:TPU:56, one launch (start us, length us, event | category | flops | bytes accessed | tf_op | source)
XLA Modules:
  0.0 57.0 jit_solution(13021318787060500659)
XLA Ops:
  0.6 53.9 %packed_attention.1 = (bf16[2,128,1024]{2,1,0:T(8,128)(2,1)}, f32[1,128]{1,0:T(1,128)}) custom-call(bf16[2,128,1024]{2,1,0:T(8,128)(2,1)} %q_hbm.1, bf16[2,128,512]{2,1,0:T(8,128)(2,1)} %k_hbm.1, bf16[2,128,512]{2,1,0:T(8,128)(2,1)} %v_hbm.1, s32[16]{0:T(128)} %doc_ref.1), custom_call_target="tpu_custom_call" | custom-call | tf_op jit(solution)/shard_map/packed_attention/pallas_call | solution.py:384
  54.6 0.0 copy-start
  54.6 1.9 %copy.8 = bf16[2,128,1024]{2,1,0:T(8,128)(2,1)} copy(bf16[2,128,1024]{2,1,0:T(8,128)(2,1)} %get-tuple-element.8) | data formatting | bytes 1048576
  56.5 0.0 copy-done
  56.5 0.5 copy.9
Async XLA Ops:
  54.6 1.9 %copy-start = (f32[1,128]{1,0:T(1,128)S(1)}, f32[1,128]{1,0:T(1,128)}, u32[]{:S(2)}) copy-start(f32[1,128]{1,0:T(1,128)} %get-tuple-element.5) | copy-start | bytes 1540

commit v3 on v2

v3 whole, which is shorter than its diff:
```python
import functools

import jax
import jax.numpy as jnp
from jax import lax
from jax.experimental import pallas as pl
from jax.experimental.pallas import tpu as pltpu
from jax.sharding import PartitionSpec as P

QH = 64
KVH = 4
HD = 128
TOKENS = 8192
MOST = 4096
NDOCS = 16

ROWS_Y = 8
HALF_Y = 4
Z_LO = 4
CORES = 2
Z_HI = 2
TP = 8
BLOCK = 128
ROW_KEYS = Z_LO * CORES * BLOCK
HEADS = QH // TP
TILE = 256

LOG2E = 1.4426950408889634
LN2 = 0.6931471805599453
LOG2_SCALE = HD**-0.5 * LOG2E
MASKED = -1e30
EMPTY = -1e35
MESH = pl.DeviceIdType.MESH


AHEAD_TOP = {
    0: (("relay", 1),),
    1: (("finish", 1), ("spread", 4),),
    2: (("relay", 2),),
    3: (("finish", 2), ("spread", 5),),
    4: (("relay", 3),),
    5: (("finish", 3),),
    6: (("spread", 6),),
    7: (("relay", 4), ("finish", 4), ("spread", 7),),
    9: (("relay", 5), ("finish", 5),),
    11: (("relay", 6), ("finish", 6),),
    13: (("relay", 7), ("finish", 7),),
}
AHEAD_LOW = {
    0: (("relay", 1),),
    1: (("finish", 1), ("spread", 4),),
    2: (("relay", 2), ("spread", 5),),
    3: (("finish", 2),),
    4: (("relay", 3),),
    5: (("finish", 3),),
    7: (("relay", 4), ("finish", 4),),
    9: (("relay", 5), ("finish", 5),),
    11: (("relay", 6), ("finish", 6),),
    13: (("relay", 7), ("finish", 7),),
}


def kernel(
    q_hbm, k_hbm, v_hbm, doc_ref, out_ref, lse_ref,
    kv, q_vm, acc, peak, total, bias, eye, scores_0, scores_1, weights_0, weights_1, factor_0, factor_1, gaps,
    load_sem, y_send, y_recv, z_send, z_recv, f_send, f_recv, s_send, s_recv, u_send, u_recv, g_send, g_recv,
):
    ctx = lax.axis_index("ctx")
    tp = lax.axis_index("tp")
    y = ctx // (Z_LO * CORES)
    z_lo = (ctx // CORES) % Z_LO
    core = ctx % CORES
    x = tp // Z_HI
    z = (tp % Z_HI) * Z_LO + z_lo
    half = y // HALF_Y
    row = y % HALF_Y
    steps = 2 * (row + 1)

    def at_z(where):
        where = (where + 2 * Z_HI * Z_LO) % (Z_HI * Z_LO)
        return (y * (Z_LO * CORES) + (where % Z_LO) * CORES + core, x * Z_HI + where // Z_LO)

    def at_row(where):
        return ((half * HALF_Y + where) * (Z_LO * CORES) + z_lo * CORES + core, tp)

    above, below = at_z(z + 1), at_z(z - 1)
    sibling = (ctx + 1 - 2 * core, tp)
    z_next, z_prev, z_far = (z_lo + 1) % Z_LO, (z_lo + 3) % Z_LO, (z_lo + 2) % Z_LO

    barrier = pltpu.get_barrier_semaphore()

    def greet(device):
        pl.semaphore_signal(barrier, inc=1, device_id=device, device_id_type=MESH)

    greet(above)
    greet(below)
    greet(at_z(z + 2))
    greet(at_z(z - 2))
    greet(sibling)
    for other in range(1, HALF_Y):
        greet(at_row((row + other) % HALF_Y))
    for other in range(1, TP):
        greet((ctx, (tp + other) % TP))

    head = pl.ds(pl.multiple_of(x * HD, HD), HD)
    loads = []
    for m in range(2):
        loads.append(pltpu.make_async_copy(k_hbm.at[m, :, head], kv.at[m, row, 0, z_lo, core], load_sem.at[m, 0]))
        loads.append(pltpu.make_async_copy(v_hbm.at[m, :, head], kv.at[m, row, 1, z_lo, core], load_sem.at[m, 1]))
    for m in range(2):
        loads.append(pltpu.make_async_copy(q_hbm.at[m], q_vm.at[m], load_sem.at[m, 2]))
    for load in loads:
        load.start()

    position = ctx * BLOCK + lax.broadcasted_iota(jnp.int32, (8, BLOCK), 1)
    begin = jnp.zeros((8, BLOCK), jnp.int32)
    end = jnp.int32(0)
    for doc in range(NDOCS):
        end = end + doc_ref[doc]
        begin = jnp.where(position >= end, end, begin)

    for load in loads[:4]:
        load.wait()
    pl.semaphore_wait(barrier, 5 + (HALF_Y - 1) + (TP - 1))

    def step_of(step):
        return step % 2, row - step // 2

    def remote(src, dst, send, recv, device):
        return pltpu.make_async_remote_copy(
            src_ref=src, dst_ref=dst, send_sem=send, recv_sem=recv, device_id=device, device_id_type=MESH
        )

    def up_copy(m, other):
        mine = kv.at[m, row, :, z_lo, core]
        return remote(mine, mine, y_send.at[m, other], y_recv.at[m, row], at_row(other))

    def up_relay(m, r):
        block = kv.at[m, r, :, z_lo, core]
        return remote(block, block, y_send.at[m, r], y_recv.at[m, r], at_row(HALF_Y - 1))

    def from_row(m, r):
        block = kv.at[m, r, :, z_lo, core]
        return remote(block, block, y_send.at[m, 0], y_recv.at[m, r], at_row(r))

    def z_copy(m, r, way):
        block = kv.at[m, r, :, z_lo, core]
        return remote(block, block, z_send.at[m, r, way], z_recv.at[m, r, way], below if way else above)

    def z_arrival(m, r, way):
        block = kv.at[m, r, :, z_next if way else z_prev, core]
        return remote(block, block, z_send.at[m, r, way], z_recv.at[m, r, way], above if way else below)

    def far_copy(m, r, way):
        block = kv.at[m, r, way, z_lo, core]
        return remote(block, block, f_send.at[m, r, way], f_recv.at[m, r, way], at_z(z - 2 if way else z + 2))

    def far_arrival(m, r, way):
        block = kv.at[m, r, way, z_far, core]
        return remote(block, block, f_send.at[m, r, way], f_recv.at[m, r, way], at_z(z + 2 if way else z - 2))

    def far_up(m):
        block = kv.at[m, row, :, z_far, core]
        return remote(block, block, u_send.at[m], u_recv.at[m, row], at_row(HALF_Y - 1))

    def far_from_row(m, r):
        block = kv.at[m, r, :, z_far, core]
        return remote(block, block, u_send.at[m], u_recv.at[m, r], at_row(r))

    top_row = row == HALF_Y - 1
    sends_far_up = row < HALF_Y - 2

    columns = (z_lo, z_prev, z_next, z_far)

    def sib_copy(m, r, kind):
        block = kv.at[m, r, :, columns[kind], core]
        return remote(block, block, s_send.at[m, r, kind], s_recv.at[m, r, kind], sibling)

    def sib_arrival(m, r, kind):
        block = kv.at[m, r, :, columns[kind], 1 - core]
        return remote(block, block, s_send.at[m, r, kind], s_recv.at[m, r, kind], sibling)

    def pass_on(m, r):
        for way in range(2):
            z_copy(m, r, way).start()
        sib_copy(m, r, 0).start()

    def far_by_z(step):
        return jnp.logical_not(top_row & (step >= 4))

    def spread(step):
        m, r = step_of(step)
        from_row(m, r).wait_recv()
        pass_on(m, r)

        @pl.when(row == HALF_Y - 2)
        def _():
            up_relay(m, r).start()

        @pl.when(far_by_z(step))
        def _():
            for way in range(2):
                far_copy(m, r, way).start()

    def relay(step):
        m, r = step_of(step)
        for way in range(2):
            z_arrival(m, r, way).wait_recv()
            sib_copy(m, r, 1 + way).start()

    def finish(step):
        m, r = step_of(step)

        @pl.when(far_by_z(step))
        def _():
            for way in range(2):
                far_arrival(m, r, way).wait_recv()

        @pl.when(jnp.logical_not(far_by_z(step)))
        def _():
            far_from_row(m, r).wait_recv()

        sib_copy(m, r, 3).start()

        @pl.when(sends_far_up & (step < 2))
        def _():
            far_up(m).start()

    def gather_done(step):
        m, r = step_of(step)
        for kind in range(4):
            sib_arrival(m, r, kind).wait_recv()

    pairs = HEADS * BLOCK // TILE // 2
    tile_heads = TILE // BLOCK
    scores, weights, factors = (scores_0, scores_1), (weights_0, weights_1), (factor_0, factor_1)

    def place(tile):
        tile = jnp.maximum(tile, 0)
        m, r = step_of(tile // (2 * pairs))
        return m, r, tile % (2 * pairs)

    def score(tile, slot):
        m, r, at = place(tile)
        heads = [
            q_vm[m, :, pl.ds(pl.multiple_of((at * tile_heads + h) * HD, HD), HD)] for h in range(tile_heads)
        ]
        q = jnp.concatenate([jnp.concatenate([h, eye[...]], axis=1) for h in heads], axis=0)
        keys = jnp.concatenate([kv[m, r, 0].reshape(ROW_KEYS, HD), bias[r]], axis=1)
        scores[slot][...] = lax.dot_general(q, keys, (((1,), (1,)), ((), ())), preferred_element_type=jnp.float32)

    def weigh(tile, slot):
        m, r, at = place(tile)
        rows = pl.ds(pl.multiple_of(at * TILE, TILE), TILE)
        here = scores[slot][...]
        old = peak[m, rows, :]
        new = jnp.maximum(old, jnp.max(here, axis=1, keepdims=True) * LOG2_SCALE)
        factors[slot][...] = jnp.exp2(old - new)
        peak[m, rows, :] = new
        weights[slot][...] = jnp.exp2(here * LOG2_SCALE - new[:, :1]).astype(jnp.bfloat16)

    def gather(tile, slot):
        m, r, at = place(tile)
        rows = pl.ds(pl.multiple_of(at * TILE, TILE), TILE)
        values = jnp.concatenate([kv[m, r, 1].reshape(ROW_KEYS, HD), jnp.ones((ROW_KEYS, 128), jnp.bfloat16)], axis=1)
        both = jnp.dot(weights[slot][...], values, preferred_element_type=jnp.float32)
        acc[m, rows, :] = acc[m, rows, :] * factors[slot][...] + both[:, :HD]
        total[m, rows, :] = total[m, rows, :] * factors[slot][...] + both[:, HD:]

    def mask_row(r, _):
        key_at = (half * HALF_Y + r) * ROW_KEYS + lax.broadcasted_iota(jnp.int32, (ROW_KEYS, BLOCK), 0)
        visible = (key_at >= begin[:1, :]) & (key_at <= position[:1, :])
        bias[r] = jnp.where(visible, 0.0, MASKED).astype(jnp.bfloat16)
        return 0

    def when_live(step, act):
        @pl.when(step < steps)
        def _():
            act(step)

    def up(m, other):
        @pl.when(other < HALF_Y)
        def _():
            up_copy(m, other).start()

    def open_row(m):
        pass_on(m, row)
        for way in range(2):
            far_copy(m, row, way).start()

    open_row(0)
    up(0, row + 1)
    up(1, row + 1)

    acc[...] = jnp.zeros_like(acc)
    total[...] = jnp.zeros_like(total)
    peak[...] = jnp.full_like(peak, MASKED)
    scores_1[...] = jnp.full_like(scores_1, EMPTY)
    for ref in (weights_0, weights_1):
        ref[...] = jnp.zeros_like(ref)
    for ref in (factor_0, factor_1):
        ref[...] = jnp.ones_like(ref)
    eye[...] = (
        lax.broadcasted_iota(jnp.int32, (BLOCK, BLOCK), 0) == lax.broadcasted_iota(jnp.int32, (BLOCK, BLOCK), 1)
    ).astype(jnp.bfloat16)

    for m in range(2):
        @pl.when(row == 0)
        def _():
            up(m, HALF_Y - 2)

    open_row(1)
    lax.fori_loop(0, row + 1, mask_row, 0)
    relay(0)
    when_live(2, spread)
    finish(0)
    when_live(3, spread)

    for load in loads[4:]:
        load.wait()

    def pair(at, _):
        for here, acts, mine in [(*item, top_row) for item in AHEAD_TOP.items()] + [
            (*item, jnp.logical_not(top_row)) for item in AHEAD_LOW.items()
        ]:
            @pl.when((at == here) & mine)
            def _():
                for act, step in acts:
                    when_live(step, {"spread": spread, "relay": relay, "finish": finish}[act])

        @pl.when(at % pairs == 0)
        def _():
            gather_done(at // pairs)

        tile = 2 * at
        score(tile, 0)
        weigh(tile - 1, 1)
        gather(tile - 2, 0)
        score(tile + 1, 1)
        weigh(tile, 0)
        gather(tile - 1, 1)
        return 0

    lax.fori_loop(0, pairs * steps, pair, 0)
    tiles = 2 * pairs * steps
    weigh(tiles - 1, 1)
    gather(tiles - 2, 0)
    gather(tiles - 1, 1)

    gap = jnp.zeros((BLOCK, 128), jnp.float32)
    for h in range(HEADS):
        rows = pl.ds(h * BLOCK, BLOCK)
        gap = gap + ((peak[0, rows, :] - peak[1, rows, :]) * LN2 + (jnp.log(total[0, rows, :]) - jnp.log(total[1, rows, :])))
    gaps[tp] = gap.T[:8, :]

    def gap_copy(other):
        return remote(gaps.at[tp], gaps.at[tp], g_send.at[other], g_recv.at[tp], (ctx, (tp + other) % TP))

    def gap_arrival(other):
        peer = (tp + other) % TP
        return remote(gaps.at[peer], gaps.at[peer], g_send.at[other], g_recv.at[peer], (ctx, peer))

    for other in range(1, TP):
        gap_copy(other).start()

    for m in range(2):
        for h in range(HEADS):
            rows = pl.ds(h * BLOCK, BLOCK)
            out_ref[m, :, pl.ds(h * HD, HD)] = (acc[m, rows, :] / total[m, rows, :]).astype(jnp.bfloat16)

    def wait_sends(step, _):
        m, r = step_of(step)
        for way in range(2):
            z_copy(m, r, way).wait_send()

        @pl.when(far_by_z(step))
        def _():
            for way in range(2):
                far_copy(m, r, way).wait_send()

        for kind in range(4):
            sib_copy(m, r, kind).wait_send()
        return 0

    lax.fori_loop(0, steps, wait_sends, 0)
    for m in range(2):
        for other in range(1, HALF_Y):
            @pl.when((other > row) & ((other < HALF_Y - 1) | (row == HALF_Y - 2)))
            def _():
                up_copy(m, other).wait_send()

        for r in range(2):
            @pl.when(row == HALF_Y - 2)
            def _():
                up_relay(m, r).wait_send()

        @pl.when(sends_far_up)
        def _():
            far_up(m).wait_send()

    for other in range(1, TP):
        gap_arrival(other).wait_recv()
    whole = gaps[0]
    for peer in range(1, TP):
        whole = whole + gaps[peer]
    lse_ref[...] = whole[:1, :] * (1.0 / QH)
    for other in range(1, TP):
        gap_copy(other).wait_send()


def per_device(queries, keys, values, doc_lengths):
    dma = pltpu.SemaphoreType.DMA
    attended, gap = pl.pallas_call(
        kernel,
        out_shape=[
            pltpu.VMEM((2, BLOCK, HEADS * HD), jnp.bfloat16),
            pltpu.VMEM((1, BLOCK), jnp.float32),
        ],
        in_specs=[pl.BlockSpec(memory_space=pl.ANY)] * 3 + [pl.BlockSpec(memory_space=pltpu.SMEM)],
        out_specs=[pl.BlockSpec(memory_space=pltpu.VMEM)] * 2,
        scratch_shapes=[
            pltpu.VMEM((2, HALF_Y, 2, Z_LO, CORES, BLOCK, HD), jnp.bfloat16),
            pltpu.VMEM((2, BLOCK, HEADS * HD), jnp.bfloat16),
            pltpu.VMEM((2, HEADS * BLOCK, HD), jnp.float32),
            pltpu.VMEM((2, HEADS * BLOCK, 128), jnp.float32),
            pltpu.VMEM((2, HEADS * BLOCK, 128), jnp.float32),
            pltpu.VMEM((HALF_Y, ROW_KEYS, BLOCK), jnp.bfloat16),
            pltpu.VMEM((BLOCK, BLOCK), jnp.bfloat16),
            pltpu.VMEM((TILE, ROW_KEYS), jnp.float32),
            pltpu.VMEM((TILE, ROW_KEYS), jnp.float32),
            pltpu.VMEM((TILE, ROW_KEYS), jnp.bfloat16),
            pltpu.VMEM((TILE, ROW_KEYS), jnp.bfloat16),
            pltpu.VMEM((TILE, 128), jnp.float32),
            pltpu.VMEM((TILE, 128), jnp.float32),
            pltpu.VMEM((TP, 8, 128), jnp.float32),
            dma((2, 3)),
            dma((2, HALF_Y)),
            dma((2, HALF_Y)),
            dma((2, HALF_Y, 2)),
            dma((2, HALF_Y, 2)),
            dma((2, HALF_Y, 2)),
            dma((2, HALF_Y, 2)),
            dma((2, HALF_Y, 4)),
            dma((2, HALF_Y, 4)),
            dma((2,)),
            dma((2, HALF_Y)),
            dma((TP,)),
            dma((TP,)),
        ],
        compiler_params=pltpu.CompilerParams(
            collective_id=0, has_side_effects=True, vmem_limit_bytes=60 * 2**20
        ),
        name="packed_attention",
    )(queries, keys, values, doc_lengths)
    return attended, gap.reshape(BLOCK)


def solution(mesh):
    in_specs = (P(None, "ctx", "tp"), P(None, "ctx", None), P(None, "ctx", None), P())
    out_specs = (P(None, "ctx", "tp"), P("ctx"))
    return jax.shard_map(
        per_device, mesh=mesh, in_specs=in_specs, out_specs=out_specs, check_vma=False
    )
```

time: 57.1 us -> 50.3 us (0.88); the launches traced: 57 us -> 49.4 us
  Pallas kernels: 53.9 us -> 47.5 us
  local copies, waits for them, and re-layouts: 2.38 us -> 1.31 us
    pallas_call x1, Pallas kernels: 53.9 us -> 47.5 us  [per_device(): pl.pallas_call(kernel, out_shape=[pltpu.VMEM((2, BLOCK, HEADS * HD), jnp....]
    unnamed x4 -> x2, local copies, waits for them, and re-layouts: 2.38 us -> 1.31 us
where the time goes in v3:
time: 50.3 us; the launch traced here: 49.4 us
  Pallas kernels  47.5 us (94%)
  local copies, waits for them, and re-layouts  1.31 us (3%)
  between operations  0.64 us (1%)
    pallas_call x1, Pallas kernels, per_device(): pl.pallas_call(kernel, out_shape=[pltpu.VMEM((2, BLOCK, HEADS * HD), jnp....  47.5 us
    unnamed x2, local copies, waits for them, and re-layouts  1.31 us

profile of v3, /device:TPU:56, one launch (start us, length us, event | category | flops | bytes accessed | tf_op | source)
XLA Modules:
  0.0 49.4 jit_solution(14810927246207521409)
XLA Ops:
  0.6 47.5 %packed_attention.1 = (bf16[2,128,1024]{2,1,0:T(8,128)(2,1)S(1)}, f32[1,128]{1,0:T(1,128)S(1)}) custom-call(bf16[2,128,1024]{2,1,0:T(8,128)(2,1)} %q_hbm.1, bf16[2,128,512]{2,1,0:T(8,128)(2,1)} %k_hbm.1, bf16[2,128,512]{2,1,0:T(8,128)(2,1)} %v_hbm.1, s32[16]{0:T(128)} %doc_ref.1), custom_call_target="tpu_custom_call" | custom-call | tf_op jit(solution)/shard_map/packed_attention/pallas_call | solution.py:413
  48.1 0.8 %copy.8 = bf16[2,128,1024]{2,1,0:T(8,128)(2,1)} copy(bf16[2,128,1024]{2,1,0:T(8,128)(2,1)S(1)} %get-tuple-element.6) | data formatting | bytes 1048576
  48.9 0.5 %copy.9 = f32[128]{0:T(128)} copy(f32[128]{0:T(128)S(1)} %bitcast.1) | data formatting | bytes 1024

commit v4 on v3

--- a/solution.py
+++ b/solution.py
@@ -33,37 +33,10 @@
 MESH = pl.DeviceIdType.MESH
 
 
-AHEAD_TOP = {
-    0: (("relay", 1),),
-    1: (("finish", 1), ("spread", 4),),
-    2: (("relay", 2),),
-    3: (("finish", 2), ("spread", 5),),
-    4: (("relay", 3),),
-    5: (("finish", 3),),
-    6: (("spread", 6),),
-    7: (("relay", 4), ("finish", 4), ("spread", 7),),
-    9: (("relay", 5), ("finish", 5),),
-    11: (("relay", 6), ("finish", 6),),
-    13: (("relay", 7), ("finish", 7),),
-}
-AHEAD_LOW = {
-    0: (("relay", 1),),
-    1: (("finish", 1), ("spread", 4),),
-    2: (("relay", 2), ("spread", 5),),
-    3: (("finish", 2),),
-    4: (("relay", 3),),
-    5: (("finish", 3),),
-    7: (("relay", 4), ("finish", 4),),
-    9: (("relay", 5), ("finish", 5),),
-    11: (("relay", 6), ("finish", 6),),
-    13: (("relay", 7), ("finish", 7),),
-}
-
-
 def kernel(
     q_hbm, k_hbm, v_hbm, doc_ref, out_ref, lse_ref,
     kv, q_vm, acc, peak, total, bias, eye, scores_0, scores_1, weights_0, weights_1, factor_0, factor_1, gaps,
-    load_sem, y_send, y_recv, z_send, z_recv, f_send, f_recv, s_send, s_recv, u_send, u_recv, g_send, g_recv,
+    load_sem, y_send, y_recv, z_send, z_recv, s_send, s_recv, u_send, g_send, g_recv,
 ):
     ctx = lax.axis_index("ctx")
     tp = lax.axis_index("tp")
@@ -85,7 +58,7 @@
 
     above, below = at_z(z + 1), at_z(z - 1)
     sibling = (ctx + 1 - 2 * core, tp)
-    z_next, z_prev, z_far = (z_lo + 1) % Z_LO, (z_lo + 3) % Z_LO, (z_lo + 2) % Z_LO
+    z_far = (z_lo + 2) % Z_LO
 
     barrier = pltpu.get_barrier_semaphore()
 
@@ -145,48 +118,37 @@
 
     def z_copy(m, r, way):
         block = kv.at[m, r, :, z_lo, core]
-        return remote(block, block, z_send.at[m, r, way], z_recv.at[m, r, way], below if way else above)
-
-    def z_arrival(m, r, way):
-        block = kv.at[m, r, :, z_next if way else z_prev, core]
-        return remote(block, block, z_send.at[m, r, way], z_recv.at[m, r, way], above if way else below)
+        return remote(block, block, z_send.at[m, r, way], z_recv.at[m, r], below if way else above)
 
     def far_copy(m, r, way):
         block = kv.at[m, r, way, z_lo, core]
-        return remote(block, block, f_send.at[m, r, way], f_recv.at[m, r, way], at_z(z - 2 if way else z + 2))
-
-    def far_arrival(m, r, way):
-        block = kv.at[m, r, way, z_far, core]
-        return remote(block, block, f_send.at[m, r, way], f_recv.at[m, r, way], at_z(z + 2 if way else z - 2))
+        return remote(block, block, z_send.at[m, r, 2 + way], z_recv.at[m, r], at_z(z - 2 if way else z + 2))
+
+    def arrival(m, r):
+        three = kv.at[m, r, :, pl.ds(0, Z_LO - 1), core]
+        return remote(three, three, z_send.at[m, r, 0], z_recv.at[m, r], above)
 
     def far_up(m):
         block = kv.at[m, row, :, z_far, core]
-        return remote(block, block, u_send.at[m], u_recv.at[m, row], at_row(HALF_Y - 1))
-
-    def far_from_row(m, r):
-        block = kv.at[m, r, :, z_far, core]
-        return remote(block, block, u_send.at[m], u_recv.at[m, r], at_row(r))
+        return remote(block, block, u_send.at[m], z_recv.at[m, row], at_row(HALF_Y - 1))
+
+    def sib_copy(m, r):
+        mine = kv.at[m, r, :, :, core]
+        return remote(mine, mine, s_send.at[m, r], s_recv.at[m, r], sibling)
+
+    def sib_arrival(m, r):
+        other = kv.at[m, r, :, :, 1 - core]
+        return remote(other, other, s_send.at[m, r], s_recv.at[m, r], sibling)
 
     top_row = row == HALF_Y - 1
     sends_far_up = row < HALF_Y - 2
 
-    columns = (z_lo, z_prev, z_next, z_far)
-
-    def sib_copy(m, r, kind):
-        block = kv.at[m, r, :, columns[kind], core]
-        return remote(block, block, s_send.at[m, r, kind], s_recv.at[m, r, kind], sibling)
-
-    def sib_arrival(m, r, kind):
-        block = kv.at[m, r, :, columns[kind], 1 - core]
-        return remote(block, block, s_send.at[m, r, kind], s_recv.at[m, r, kind], sibling)
+    def far_by_z(step):
+        return jnp.logical_not(top_row & (step >= 4))
 
     def pass_on(m, r):
         for way in range(2):
             z_copy(m, r, way).start()
-        sib_copy(m, r, 0).start()
-
-    def far_by_z(step):
-        return jnp.logical_not(top_row & (step >= 4))
 
     def spread(step):
         m, r = step_of(step)
@@ -202,25 +164,10 @@
             for way in range(2):
                 far_copy(m, r, way).start()
 
-    def relay(step):
+    def arrive(step):
         m, r = step_of(step)
-        for way in range(2):
-            z_arrival(m, r, way).wait_recv()
-            sib_copy(m, r, 1 + way).start()
-
-    def finish(step):
-        m, r = step_of(step)
-
-        @pl.when(far_by_z(step))
-        def _():
-            for way in range(2):
-                far_arrival(m, r, way).wait_recv()
-
-        @pl.when(jnp.logical_not(far_by_z(step)))
-        def _():
-            far_from_row(m, r).wait_recv()
-
-        sib_copy(m, r, 3).start()
+        arrival(m, r).wait_recv()
+        sib_copy(m, r).start()
 
         @pl.when(sends_far_up & (step < 2))
         def _():
@@ -228,8 +175,7 @@
 
     def gather_done(step):
         m, r = step_of(step)
-        for kind in range(4):
-            sib_arrival(m, r, kind).wait_recv()
+        sib_arrival(m, r).wait_recv()
 
     pairs = HEADS * BLOCK // TILE // 2
     tile_heads = TILE // BLOCK
@@ -275,6 +221,11 @@
 
     def when_live(step, act):
         @pl.when(step < steps)
+        def _():
+            act(step)
+
+    def when_live_after_own(step, act):
+        @pl.when((step >= 4) & (step < steps))
         def _():
             act(step)
 
@@ -311,37 +262,30 @@
 
     open_row(1)
     lax.fori_loop(0, row + 1, mask_row, 0)
-    relay(0)
     when_live(2, spread)
-    finish(0)
+    arrive(0)
     when_live(3, spread)
 
     for load in loads[4:]:
         load.wait()
 
-    def pair(at, _):
-        for here, acts, mine in [(*item, top_row) for item in AHEAD_TOP.items()] + [
-            (*item, jnp.logical_not(top_row)) for item in AHEAD_LOW.items()
-        ]:
-            @pl.when((at == here) & mine)
-            def _():
-                for act, step in acts:
-                    when_live(step, {"spread": spread, "relay": relay, "finish": finish}[act])
-
-        @pl.when(at % pairs == 0)
-        def _():
-            gather_done(at // pairs)
-
-        tile = 2 * at
+    def two_tiles(tile):
         score(tile, 0)
         weigh(tile - 1, 1)
         gather(tile - 2, 0)
         score(tile + 1, 1)
         weigh(tile, 0)
         gather(tile - 1, 1)
+
+    def whole_step(step, _):
+        gather_done(step)
+        when_live_after_own(step + 3, spread)
+        two_tiles(2 * pairs * step)
+        when_live(step + 1, arrive)
+        two_tiles(2 * pairs * step + 2)
         return 0
 
-    lax.fori_loop(0, pairs * steps, pair, 0)
+    lax.fori_loop(0, steps, whole_step, 0)
     tiles = 2 * pairs * steps
     weigh(tiles - 1, 1)
     gather(tiles - 2, 0)
@@ -372,14 +316,13 @@
         m, r = step_of(step)
         for way in range(2):
             z_copy(m, r, way).wait_send()
+        sib_copy(m, r).wait_send()
 
         @pl.when(far_by_z(step))
         def _():
             for way in range(2):
                 far_copy(m, r, way).wait_send()
 
-        for kind in range(4):
-            sib_copy(m, r, kind).wait_send()
         return 0
 
     lax.fori_loop(0, steps, wait_sends, 0)
@@ -436,14 +379,11 @@
             dma((2, 3)),
             dma((2, HALF_Y)),
             dma((2, HALF_Y)),
-            dma((2, HALF_Y, 2)),
-            dma((2, HALF_Y, 2)),
-            dma((2, HALF_Y, 2)),
-            dma((2, HALF_Y, 2)),
             dma((2, HALF_Y, 4)),
-            dma((2, HALF_Y, 4)),
+            dma((2, HALF_Y)),
+            dma((2, HALF_Y)),
+            dma((2, HALF_Y)),
             dma((2,)),
-            dma((2, HALF_Y)),
             dma((TP,)),
             dma((TP,)),
         ],

time: 50.3 us -> 48.7 us (0.968); the launches traced: 49.4 us -> 48.5 us
  Pallas kernels: 47.5 us -> 46.6 us
    pallas_call x1, Pallas kernels: 47.5 us -> 46.6 us  [per_device(): pl.pallas_call(kernel, out_shape=[pltpu.VMEM((2, BLOCK, HEADS * HD), jnp....]
where the time goes in v4:
time: 48.7 us; the launch traced here: 48.5 us
  Pallas kernels  46.6 us (96%)
  local copies, waits for them, and re-layouts  1.31 us (3%)
  between operations  0.64 us (1%)
    pallas_call x1, Pallas kernels, per_device(): pl.pallas_call(kernel, out_shape=[pltpu.VMEM((2, BLOCK, HEADS * HD), jnp....  46.6 us
    unnamed x2, local copies, waits for them, and re-layouts  1.31 us

profile of v4, /device:TPU:56, one launch (start us, length us, event | category | flops | bytes accessed | tf_op | source)
XLA Modules:
  0.0 48.5 jit_solution(3113449968987579286)
XLA Ops:
  0.6 46.6 %packed_attention.1 = (bf16[2,128,1024]{2,1,0:T(8,128)(2,1)S(1)}, f32[1,128]{1,0:T(1,128)S(1)}) custom-call(bf16[2,128,1024]{2,1,0:T(8,128)(2,1)} %q_hbm.1, bf16[2,128,512]{2,1,0:T(8,128)(2,1)} %k_hbm.1, bf16[2,128,512]{2,1,0:T(8,128)(2,1)} %v_hbm.1, s32[16]{0:T(128)} %doc_ref.1), custom_call_target="tpu_custom_call" | custom-call | tf_op jit(solution)/shard_map/packed_attention/pallas_call | solution.py:356
  47.2 0.8 %copy.8 = bf16[2,128,1024]{2,1,0:T(8,128)(2,1)} copy(bf16[2,128,1024]{2,1,0:T(8,128)(2,1)S(1)} %get-tuple-element.6) | data formatting | bytes 1048576
  48.0 0.5 %copy.9 = f32[128]{0:T(128)} copy(f32[128]{0:T(128)S(1)} %bitcast.1) | data formatting | bytes 1024

commit v5 on v4

--- a/solution.py
+++ b/solution.py
@@ -279,9 +279,9 @@
 
     def whole_step(step, _):
         gather_done(step)
-        when_live_after_own(step + 3, spread)
         two_tiles(2 * pairs * step)
         when_live(step + 1, arrive)
+        when_live_after_own(step + 3, spread)
         two_tiles(2 * pairs * step + 2)
         return 0
 

time: 48.7 us -> 48.1 us (0.988)
  Pallas kernels: 46.6 us -> 46 us
    pallas_call x1, Pallas kernels: 46.6 us -> 46 us  [per_device(): pl.pallas_call(kernel, out_shape=[pltpu.VMEM((2, BLOCK, HEADS * HD), jnp....]
where the time goes in v5:
time: 48.1 us; the launch traced here: 47.9 us
  Pallas kernels  46 us (96%)
  local copies, waits for them, and re-layouts  1.31 us (3%)
  between operations  0.64 us (1%)
    pallas_call x1, Pallas kernels, per_device(): pl.pallas_call(kernel, out_shape=[pltpu.VMEM((2, BLOCK, HEADS * HD), jnp....  46 us
    unnamed x2, local copies, waits for them, and re-layouts  1.31 us

profile of v5, /device:TPU:56, one launch (start us, length us, event | category | flops | bytes accessed | tf_op | source)
XLA Modules:
  0.0 47.9 jit_solution(12917877215335102483)
XLA Ops:
  0.6 46.0 %packed_attention.1 = (bf16[2,128,1024]{2,1,0:T(8,128)(2,1)S(1)}, f32[1,128]{1,0:T(1,128)S(1)}) custom-call(bf16[2,128,1024]{2,1,0:T(8,128)(2,1)} %q_hbm.1, bf16[2,128,512]{2,1,0:T(8,128)(2,1)} %k_hbm.1, bf16[2,128,512]{2,1,0:T(8,128)(2,1)} %v_hbm.1, s32[16]{0:T(128)} %doc_ref.1), custom_call_target="tpu_custom_call" | custom-call | tf_op jit(solution)/shard_map/packed_attention/pallas_call | solution.py:356
  46.6 0.8 %copy.8 = bf16[2,128,1024]{2,1,0:T(8,128)(2,1)} copy(bf16[2,128,1024]{2,1,0:T(8,128)(2,1)S(1)} %get-tuple-element.6) | data formatting | bytes 1048576
  47.4 0.5 %copy.9 = f32[128]{0:T(128)} copy(f32[128]{0:T(128)S(1)} %bitcast.1) | data formatting | bytes 1024

commit v6 on v5

--- a/solution.py
+++ b/solution.py
@@ -30,6 +30,7 @@
 LOG2_SCALE = HD**-0.5 * LOG2E
 MASKED = -1e30
 EMPTY = -1e35
+FAR_FIRST = (5, 3, 1, 7, 4, 2, 6)
 MESH = pl.DeviceIdType.MESH
 
 
@@ -65,6 +66,8 @@
     def greet(device):
         pl.semaphore_signal(barrier, inc=1, device_id=device, device_id_type=MESH)
 
+    for other in FAR_FIRST:
+        greet((ctx, (tp + other) % TP))
     greet(above)
     greet(below)
     greet(at_z(z + 2))
@@ -72,8 +75,6 @@
     greet(sibling)
     for other in range(1, HALF_Y):
         greet(at_row((row + other) % HALF_Y))
-    for other in range(1, TP):
-        greet((ctx, (tp + other) % TP))
 
     head = pl.ds(pl.multiple_of(x * HD, HD), HD)
     loads = []
@@ -304,7 +305,7 @@
         peer = (tp + other) % TP
         return remote(gaps.at[peer], gaps.at[peer], g_send.at[other], g_recv.at[peer], (ctx, peer))
 
-    for other in range(1, TP):
+    for other in FAR_FIRST:
         gap_copy(other).start()
 
     for m in range(2):

time: 48.1 us -> 47.9 us (level)
  no operation moved by 1% of the time
where the time goes in v6:
time: 47.9 us; the launch traced here: 47.8 us
  Pallas kernels  45.9 us (96%)
  local copies, waits for them, and re-layouts  1.31 us (3%)
  between operations  0.64 us (1%)
    pallas_call x1, Pallas kernels, per_device(): pl.pallas_call(kernel, out_shape=[pltpu.VMEM((2, BLOCK, HEADS * HD), jnp....  45.9 us
    unnamed x2, local copies, waits for them, and re-layouts  1.31 us

profile of v6, /device:TPU:56, one launch (start us, length us, event | category | flops | bytes accessed | tf_op | source)
XLA Modules:
  0.0 47.8 jit_solution(15946427876275755571)
XLA Ops:
  0.6 45.9 %packed_attention.1 = (bf16[2,128,1024]{2,1,0:T(8,128)(2,1)S(1)}, f32[1,128]{1,0:T(1,128)S(1)}) custom-call(bf16[2,128,1024]{2,1,0:T(8,128)(2,1)} %q_hbm.1, bf16[2,128,512]{2,1,0:T(8,128)(2,1)} %k_hbm.1, bf16[2,128,512]{2,1,0:T(8,128)(2,1)} %v_hbm.1, s32[16]{0:T(128)} %doc_ref.1), custom_call_target="tpu_custom_call" | custom-call | tf_op jit(solution)/shard_map/packed_attention/pallas_call | solution.py:357
  46.5 0.8 %copy.8 = bf16[2,128,1024]{2,1,0:T(8,128)(2,1)} copy(bf16[2,128,1024]{2,1,0:T(8,128)(2,1)S(1)} %get-tuple-element.6) | data formatting | bytes 1048576
  47.3 0.5 %copy.9 = f32[128]{0:T(128)} copy(f32[128]{0:T(128)S(1)} %bitcast.1) | data formatting | bytes 1024
